TPU v7x, 32 devices: a whole 2x2x4 slice. The times are simulated.
32 devices in a mesh: ctx: 8 (over z, y), seq: 4 (over x, core).
Axes of the slice: x: 2, y: 2, z: 4, core: 2. Of those that a mesh axis runs over, the one named last changes fastest.
Arguments:
- query_input: bfloat16 [4, 1024, 2048], P('seq', 'ctx'), may hold values from -6 to 6
- key_input: bfloat16 [4, 1024, 2048], P('seq', 'ctx'), may hold values from -6 to 6
- value_input: bfloat16 [4, 1024, 2048], P('seq', 'ctx'), may hold values from -6 to 6
- cotangent: bfloat16 [4, 1024, 2048], P('seq', 'ctx'), may hold values from -6 to 6
- residues: float32 [2048, 16], replicated, may hold values from -1.5 to 1.5
- decay_rates: float32 [2048, 16], replicated, as said below
Outputs:
- output: bfloat16 [4, 1024, 2048], P('seq', 'ctx')
- grad_query: bfloat16 [4, 1024, 2048], P('seq', 'ctx')
- grad_key: bfloat16 [4, 1024, 2048], P('seq', 'ctx')
- grad_value: bfloat16 [4, 1024, 2048], P('seq', 'ctx')
- grad_residues: float32 [2048, 16], replicated
Inputs may be any that keep to these rules, and one draw needn't show every extreme that they name: `decay_rates`: every rate lies between 0.1 divided by 1024 and 1 divided by 30.
All inputs are finite; a program needn't handle non-finite values.
Results may differ from a plain program's by a relative error of at most 0.0013.
Values sent between devices are 32-bit elements; how exact they have to be, the bound alone decides.
A program may use at most 192 MiB of HBM per device.

v0:
```python
import math

import jax
import jax.numpy as jnp
from jax import lax
from jax.sharding import PartitionSpec as P

HIGH = lax.Precision.HIGHEST


def phase_of(count, modulus):
    wrapped = (count + modulus // 2) % modulus - modulus // 2
    return 2.0 * math.pi / modulus * wrapped.astype(jnp.float32)


def complex_apply(joined, cosines, sines, real_part, imag_part):
    table = jnp.stack(
        [jnp.stack([cosines, -sines], axis=1), jnp.stack([sines, cosines], axis=1)], axis=0
    )
    stacked = jnp.stack([real_part, imag_part], axis=0)
    product = jnp.einsum(joined, table, stacked, precision=HIGH)
    return (product[0], product[1])


def factor_pair(length):
    first_len = math.isqrt(length)
    while length % first_len:
        first_len -= 1
    return (first_len, length // first_len)


def forward_rows(real_part, imag_part):
    leading, length, columns = real_part.shape
    first_len, second_len = factor_pair(length)
    real_grid = real_part.reshape(leading, second_len, first_len, columns)
    imag_grid = imag_part.reshape(leading, second_len, first_len, columns)
    outer_steps = jnp.arange(second_len, dtype=jnp.int32)
    inner_steps = jnp.arange(first_len, dtype=jnp.int32)
    angles = phase_of(outer_steps[:, None] * outer_steps[None, :], second_len)
    real_grid, imag_grid = complex_apply(
        "pgqb,qfbak->pfgak", jnp.cos(angles), -jnp.sin(angles), real_grid, imag_grid
    )
    twist = phase_of(outer_steps[:, None] * inner_steps[None, :], length)[None, :, :, None]
    twist_cos = jnp.cos(twist)
    twist_sin = -jnp.sin(twist)
    real_grid, imag_grid = (
        real_grid * twist_cos - imag_grid * twist_sin,
        real_grid * twist_sin + imag_grid * twist_cos,
    )
    angles = phase_of(inner_steps[:, None] * inner_steps[None, :], first_len)
    real_grid, imag_grid = complex_apply(
        "phqa,qfgak->pfhgk", jnp.cos(angles), -jnp.sin(angles), real_grid, imag_grid
    )
    return (
        real_grid.reshape(leading, length, columns),
        imag_grid.reshape(leading, length, columns),
    )


def inverse_rows(real_part, imag_part):
    leading, length, columns = real_part.shape
    first_len, second_len = factor_pair(length)
    real_grid = real_part.reshape(leading, first_len, second_len, columns)
    imag_grid = imag_part.reshape(leading, first_len, second_len, columns)
    outer_steps = jnp.arange(second_len, dtype=jnp.int32)
    inner_steps = jnp.arange(first_len, dtype=jnp.int32)
    angles = phase_of(inner_steps[:, None] * inner_steps[None, :], first_len)
    real_grid, imag_grid = complex_apply(
        "paqh,qfhgk->pfagk", jnp.cos(angles), jnp.sin(angles), real_grid, imag_grid
    )
    twist = phase_of(inner_steps[:, None] * outer_steps[None, :], length)[None, :, :, None]
    twist_cos = jnp.cos(twist)
    twist_sin = jnp.sin(twist)
    real_grid, imag_grid = (
        real_grid * twist_cos - imag_grid * twist_sin,
        real_grid * twist_sin + imag_grid * twist_cos,
    )
    angles = phase_of(outer_steps[:, None] * outer_steps[None, :], second_len)
    real_grid, imag_grid = complex_apply(
        "pbqg,qfagk->pfbak", jnp.cos(angles), jnp.sin(angles), real_grid, imag_grid
    )
    return (
        real_grid.reshape(leading, length, columns),
        imag_grid.reshape(leading, length, columns),
    )


def spectrum(signal, ctx_count, ctx_rank):
    length, columns = signal.shape
    row_count = length // ctx_count
    modulus = 2 * ctx_count * length
    spread = lax.all_to_all(
        signal.reshape(ctx_count, row_count, columns),
        "ctx",
        split_axis=0,
        concat_axis=0,
        tiled=True,
    )
    freq_steps = jnp.arange(2 * ctx_count, dtype=jnp.int32)
    source_steps = jnp.arange(ctx_count, dtype=jnp.int32)
    angles = phase_of(freq_steps[:, None] * source_steps[None, :], 2 * ctx_count)
    real_part = jnp.einsum("fj,jrk->frk", jnp.cos(angles), spread, precision=HIGH)
    imag_part = -jnp.einsum("fj,jrk->frk", jnp.sin(angles), spread, precision=HIGH)
    place = ctx_rank * row_count + jnp.arange(row_count, dtype=jnp.int32)
    twist = phase_of(freq_steps[:, None] * place[None, :], modulus)[:, :, None]
    twist_cos = jnp.cos(twist)
    twist_sin = jnp.sin(twist)
    turned_real = real_part * twist_cos + imag_part * twist_sin
    turned_imag = imag_part * twist_cos - real_part * twist_sin
    moved = lax.all_to_all(
        jnp.concatenate([turned_real, turned_imag], axis=2),
        "ctx",
        split_axis=0,
        concat_axis=1,
        tiled=True,
    )
    return forward_rows(moved[..., :columns], moved[..., columns:])


def to_signal(real_part, imag_part, ctx_count, ctx_rank):
    leading, length, columns = real_part.shape
    modulus = 2 * ctx_count * length
    back_real, back_imag = inverse_rows(real_part, imag_part)
    freq_here = 2 * ctx_rank + jnp.arange(2, dtype=jnp.int32)
    place = jnp.arange(length, dtype=jnp.int32)
    twist = phase_of(freq_here[:, None] * place[None, :], modulus)[:, :, None]
    twist_cos = jnp.cos(twist)
    twist_sin = jnp.sin(twist)
    turned_real = back_real * twist_cos - back_imag * twist_sin
    turned_imag = back_real * twist_sin + back_imag * twist_cos
    returned = lax.all_to_all(
        jnp.concatenate([turned_real, turned_imag], axis=2),
        "ctx",
        split_axis=1,
        concat_axis=0,
        tiled=True,
    )
    freq_steps = jnp.arange(2 * ctx_count, dtype=jnp.int32)
    target_steps = jnp.arange(ctx_count, dtype=jnp.int32)
    angles = phase_of(target_steps[:, None] * freq_steps[None, :], 2 * ctx_count)
    rebuilt = (
        jnp.einsum("jf,frk->jrk", jnp.cos(angles), returned[..., :columns], precision=HIGH)
        - jnp.einsum("jf,frk->jrk", jnp.sin(angles), returned[..., columns:], precision=HIGH)
    ) / modulus
    arrived = lax.all_to_all(rebuilt, "ctx", split_axis=0, concat_axis=0, tiled=True)
    return arrived.reshape(length, columns)


def filter_terms(
    mix_real, mix_imag, adj_real, adj_imag, residues, decay_rates, scaling, ctx_count, ctx_rank
):
    leading, length, channels = mix_real.shape
    modulus = 2 * ctx_count * length
    seq_length = float(ctx_count * length)
    freq_index = (2 * ctx_rank + jnp.arange(2, dtype=jnp.int32))[
        :, None
    ] + 2 * ctx_count * jnp.arange(length, dtype=jnp.int32)[None, :]
    theta = phase_of(freq_index, modulus)[None, :, :, None]
    sin_theta = jnp.sin(theta)
    half_sin = jnp.sin(0.5 * theta)
    lifted = 2.0 * half_sin * half_sin
    parity = jnp.array([1.0, -1.0], jnp.float32)[None, :, None, None]
    cross_real = adj_real * mix_real + adj_imag * mix_imag
    cross_imag = adj_imag * mix_real - adj_real * mix_imag
    rate = decay_rates.T[:, None, None, :]
    lam = jnp.exp(-rate)
    numer = 1.0 - jnp.exp(-rate * seq_length) * parity
    den_real = -jnp.expm1(-rate) + lam * lifted
    den_imag = lam * sin_theta
    ratio = numer / (den_real * den_real + den_imag * den_imag)
    geo_real = den_real * ratio
    geo_imag = -den_imag * ratio
    weight = (residues * scaling).T[:, None, None, :]
    filt_real = jnp.sum(weight * geo_real, axis=0)
    filt_imag = jnp.sum(weight * geo_imag, axis=0)
    columns = jnp.sum(cross_real[None] * geo_real + cross_imag[None] * geo_imag, axis=(1, 2))
    filter_part = columns.T * scaling / modulus
    return (filt_real, filt_imag, filter_part)


def spectral_pass(mixed, adjoint, residues, decay_rates, scaling):
    ctx_count = lax.axis_size("ctx")
    ctx_rank = lax.axis_index("ctx")
    channels = mixed.shape[1]
    spec_real, spec_imag = spectrum(jnp.concatenate([mixed, adjoint], axis=1), ctx_count, ctx_rank)
    mix_real = spec_real[..., :channels]
    mix_imag = spec_imag[..., :channels]
    adj_real = spec_real[..., channels:]
    adj_imag = spec_imag[..., channels:]
    filt_real, filt_imag, filter_part = filter_terms(
        mix_real, mix_imag, adj_real, adj_imag, residues, decay_rates, scaling, ctx_count, ctx_rank
    )
    out_real = jnp.concatenate(
        [filt_real * mix_real - filt_imag * mix_imag, filt_real * adj_real + filt_imag * adj_imag],
        axis=2,
    )
    out_imag = jnp.concatenate(
        [filt_real * mix_imag + filt_imag * mix_real, filt_real * adj_imag - filt_imag * adj_real],
        axis=2,
    )
    signal = to_signal(out_real, out_imag, ctx_count, ctx_rank)
    return (signal[:, :channels], signal[:, channels:], filter_part)


def on_device(query_input, key_input, value_input, cotangent, residues, decay_rates):
    query_wide = query_input[0].astype(jnp.float32)
    key_wide = key_input[0].astype(jnp.float32)
    value_wide = value_input[0].astype(jnp.float32)
    cot_wide = cotangent[0].astype(jnp.float32)
    length = query_wide.shape[0]
    mixed = key_wide * value_wide
    adjoint = cot_wide * query_wide
    scaling = jnp.sqrt(-jnp.expm1(-2.0 * decay_rates))
    convolved, grad_mixed, filter_part = spectral_pass(
        mixed, adjoint, residues, decay_rates, scaling
    )
    summed = lax.psum(filter_part, ("ctx", "seq"))
    grad_residues = summed / float(length * lax.axis_size("ctx") * lax.axis_size("seq"))
    output = (query_wide * convolved).astype(jnp.bfloat16)[None]
    grad_query = (cot_wide * convolved).astype(jnp.bfloat16)[None]
    grad_key = (grad_mixed * value_wide).astype(jnp.bfloat16)[None]
    grad_value = (grad_mixed * key_wide).astype(jnp.bfloat16)[None]
    return (output, grad_query, grad_key, grad_value, grad_residues)


def solution(mesh):
    return jax.shard_map(
        on_device,
        mesh=mesh,
        in_specs=(
            P("seq", "ctx", None),
            P("seq", "ctx", None),
            P("seq", "ctx", None),
            P("seq", "ctx", None),
            P(),
            P(),
        ),
        out_specs=(
            P("seq", "ctx", None),
            P("seq", "ctx", None),
            P("seq", "ctx", None),
            P("seq", "ctx", None),
            P(),
        ),
        check_vma=False,
    )
```

profile of v0, /device:TPU:0, one launch (start us, length us, event | category | flops | bytes accessed | tf_op | source)
XLA Modules:
  0.0 787.4 jit_solution(15041619976937396301)
XLA Ops:
  11.3 7.3 all-to-all-start
  18.7 48.1 %all-to-all-done = f32[8,16,4096]{2,1,0:T(8,128)S(1)} async-done(((f32[8,16,4096]{2,1,0:T(8,128)}), f32[8,16,4096]{2,1,0:T(8,128)S(1)}, u32[]{:S(2)}, u32[]{:S(2)}) %all-to-all-start) | async-done | bytes 2097184 | tf_op jit(solution)/shard_map/all_to_all | solution.py:92
  66.8 4.3 fusion.29
  71.1 7.4 multiply_add_fusion.3
  78.6 4.0 pad_maximum_fusion
  82.6 8.1 %copy.74 = f32[16,16,8192]{2,1,0:T(8,128)} copy(f32[16,16,8192]{2,0,1:T(8,128)S(1)} %pad_maximum_fusion) | data formatting | bytes 16777216 | tf_op jit(solution)/shard_map/concatenate | solution.py:111
  90.7 5.5 all-to-all-start.1
  97.3 180.6 %all-to-all-done.1 = f32[16,16,8192]{2,1,0:T(8,128)} async-done(((f32[16,16,8192]{2,1,0:T(8,128)}), f32[16,16,8192]{2,1,0:T(8,128)}, u32[]{:S(2)}, u32[]{:S(2)}) %all-to-all-start.1) | async-done | bytes 8388640 | tf_op jit(solution)/shard_map/all_to_all | solution.py:110
  278.0 3.9 copy.75
  287.8 11.5 %fusion.21 = f32[2,2,16,8,4096]{4,2,0,3,1:T(8,128)S(1)} fusion(f32[1,2,16,8,4096]{4,2,0,3,1:T(8,128)S(1)} %copy.77, f32[1,2,16,8,4096]{4,2,0,3,1:T(8,128)S(1)} %copy.76, f32[1,16,2,16]{3,1,2,0:T(8,128)S(1)} %get-tuple-element.37, f32[1,16,2,16]{3,1,2,0:T(8,128)S(1)} %get-tuple-element.40), kind=kOutput, calls=%fused_computation.29 | convolution fusion | flops 807404544 | bytes 16781312 | tf_op jit(solution)/shard_map/pgqb,qfbak->pfgak/dot_general | solution.py:21
  302.1 15.9 %fusion.14 = f32[2,2,8,16,4096]{4,2,0,3,1:T(8,128)S(1)} fusion(f32[2,2,16,8,4096,1]{4,2,0,3,1,5:T(8,128)S(1)} %maximum_bitcast_fusion.2, f32[1,8,2,8]{3,1,2,0:T(8,128)S(1)} %get-tuple-element.43, f32[1,8,2,8]{3,1,2,0:T(8,128)S(1)} %get-tuple-element.46), kind=kOutput, calls=%fused_computation.26 | convolution fusion | flops 402653440 | bytes 16778240 | tf_op jit(solution)/shard_map/phqa,qfgak->pfhgk/dot_general | solution.py:21
  325.3 23.0 %multiply_reduce_fusion.1 = (f32[2,128,2048]{2,1,0:T(8,128)S(1)}, f32[2,128,2048]{2,1,0:T(8,128)S(1)}, f32[16,2048]{1,0:T(8,128)S(1)}) fusion(f32[2,128]{1,0:T(2,128)S(1)} %get-tuple-element.49, f32[16,2048]{1,0:T(8,128)S(1)} %get-tuple-element.33, f32[16,2048]{1,0:T(8,128)S(1)} %get-tuple-element.35, f32[2,128]{1,0:T(2,128)S(1)} %get-tuple-element.48, ...), kind=kLoop, calls=%fused_computation.7 | loop fusion | flops 149913600 | bytes 9177088 | tf_op jit(solution)/shard_map/reduce_sum | solution.py:174
  356.1 11.9 %fusion.20 = f32[2,2,8,16,4096]{4,2,0,3,1:T(8,128)S(1)} fusion(f32[1,2,8,16,4096]{4,2,0,3,1:T(8,128)S(1)} %copy.82, f32[1,2,8,16,4096]{4,2,0,3,1:T(8,128)S(1)} %copy.81, f32[1,8,2,8]{3,1,2,0:T(8,128)S(1)} %get-tuple-element.47, f32[1,8,2,8]{3,1,2,0:T(8,128)S(1)} %get-tuple-element.42), kind=kOutput, calls=%fused_computation.28 | convolution fusion | flops 404750592 | bytes 16778240 | tf_op jit(solution)/shard_map/paqh,qfhgk->pfagk/dot_general | solution.py:21
  370.8 16.3 %fusion.17 = f32[2,2,16,8,4096]{4,2,0,3,1:T(8,128)S(1)} fusion(f32[2,2,8,16,4096,1]{4,2,0,3,1,5:T(8,128)S(1)} %maximum_bitcast_fusion.5, f32[1,16,2,16]{3,1,2,0:T(8,128)S(1)} %get-tuple-element.41, f32[1,16,2,16]{3,1,2,0:T(8,128)S(1)} %get-tuple-element.36), kind=kOutput, calls=%fused_computation.27 | convolution fusion | flops 805307392 | bytes 16781312 | tf_op jit(solution)/shard_map/pbqg,qfagk->pfbak/dot_general | solution.py:21
  388.1 8.0 %fusion.26 = (f32[2,128,4096]{2,1,0:T(8,128)S(1)}, f32[2,128,4096]{2,1,0:T(8,128)}) fusion(f32[1,2,16,8,4096]{4,2,0,3,1:T(8,128)S(1)} %get-tuple-element.21, f32[1,2,16,8,4096]{4,2,0,3,1:T(8,128)S(1)} %get-tuple-element.20, f32[2,128]{1,0:T(2,128)S(1)} %get-tuple-element.51, f32[2,128]{1,0:T(2,128)S(1)} %get-tuple-element.50), kind=kLoop, calls=%fused_computation.42 | loop fusion | flops 6291456 | bytes 16779264 | tf_op jit(solution)/shard_map/sub | solution.py:129
  399.0 7.8 copy.88
  406.8 186.6 %all_to_all.46 = f32[2,128,8192]{2,0,1:T(2,128)S(1)} all-to-all(f32[2,128,8192]{2,0,1:T(2,128)S(1)} %copy.88), channel_id=1, replica_groups=mesh['ctx'=8,'seq'=4] {'ctx'}, dimensions={1} | all-to-all | bytes 16777216 | tf_op jit(solution)/shard_map/all_to_all | solution.py:131
  593.4 4.9 copy.89
  598.3 7.7 copy.90
  605.9 10.8 %all_to_all.40 = f32[16,16,8192]{2,0,1:T(8,128)} reshape(f32[8,2,16,8192]{3,1,0,2:T(2,128)} %copy.90) | data formatting | bytes 16777216 | tf_op jit(solution)/shard_map/all_to_all | solution.py:131
  616.8 3.9 fusion.24
  620.7 4.0 fusion.22
  627.2 3.6 all-to-all-start.3
  631.7 144.2 %all-reduce.2.cloned.1.call-done = f32[2048,16]{0,1:T(8,128)} async-done(((f32[2048,16]{0,1:T(8,128)}), f32[2048,16]{0,1:T(8,128)}) %all-reduce.2.cloned.1.call-update) | async-done | bytes 131088 | tf_op jit(solution)/shard_map/psum | solution.py:217
  (56 shorter events, 43.5 us)
Async XLA Ops:
  11.3 55.5 %all-to-all-start = ((f32[8,16,4096]{2,1,0:T(8,128)}), f32[8,16,4096]{2,1,0:T(8,128)S(1)}, u32[]{:S(2)}, u32[]{:S(2)}) async-start(f32[8,16,4096]{2,1,0:T(8,128)} %pad_maximum_fusion.4), calls=%async_computation | async-start | bytes 4194304 | tf_op jit(solution)/shard_map/all_to_all | solution.py:92
  90.7 6.3 copy-start.2
  90.7 6.3 copy-start.3
  90.7 6.4 copy-start.4
  90.7 187.3 %all-to-all-start.1 = ((f32[16,16,8192]{2,1,0:T(8,128)}), f32[16,16,8192]{2,1,0:T(8,128)}, u32[]{:S(2)}, u32[]{:S(2)}) async-start(f32[16,16,8192]{2,1,0:T(8,128)} %copy.74), calls=%async_computation.1 | async-start | bytes 16777216 | tf_op jit(solution)/shard_map/all_to_all | solution.py:110
  624.6 152.8 %copy-start = (bf16[1,128,2048]{2,1,0:T(8,128)(2,1)S(1)}, bf16[1,128,2048]{2,1,0:T(8,128)(2,1)}, u32[]{:S(2)}) copy-start(bf16[1,128,2048]{2,1,0:T(8,128)(2,1)} %param.8) | copy-start | bytes 1572868
  624.7 152.8 %copy-start.1 = (bf16[1,128,2048]{2,1,0:T(8,128)(2,1)S(1)}, bf16[1,128,2048]{2,1,0:T(8,128)(2,1)}, u32[]{:S(2)}) copy-start(bf16[1,128,2048]{2,1,0:T(8,128)(2,1)} %param.7) | copy-start | bytes 1572868
  627.2 150.2 %all-to-all-start.3 = ((f32[8,16,4096]{2,1,0:T(8,128)}), f32[8,16,4096]{2,1,0:T(8,128)S(1)}, u32[]{:S(2)}, u32[]{:S(2)}) async-start(f32[8,16,4096]{2,1,0:T(8,128)} %copy.91), calls=%async_computation.3 | async-start | bytes 4194304 | tf_op jit(solution)/shard_map/all_to_all | solution.py:145
  630.8 145.0 %all-reduce.2.cloned.1.call-start = ((), (), s32[]{:S(2)}) async-start(), calls=%async_computation.4 | async-start | bytes 262144 | tf_op jit(solution)/shard_map/psum | solution.py:217
Sparse Core Ops, SparseCore 0:
  637.8 138.0 all-reduce.1
where the time goes:
time: 794 us; the launch traced here: 787 us
  waiting for transfers between devices  373 us (47%)
  blocking collectives  187 us (24%)
  matrix products  75.1 us (9%)
  local copies, waits for them, and re-layouts  63.4 us (8%)
  other arithmetic  58.2 us (7%)
  starting transfers between devices  16.4 us (2%)
  between operations  14.6 us (2%)
    all_to_all x1, blocking collectives, to_signal(): lax.all_to_all(jnp.concatenate([turned_real, turned_imag], axis=2), 'ctx'...  187 us
    all_to_all x1, waiting for transfers between devices, spectrum(): lax.all_to_all(jnp.concatenate([turned_real, turned_imag], axis=2), 'ctx'...  181 us
    psum x1, waiting for transfers between devices, on_device(): summed = lax.psum(filter_part, ('ctx', 'seq'))  144 us
    dot_general x4, matrix products, complex_apply(): product = jnp.einsum(joined, table, stacked, precision=HIGH)  55.5 us
    all_to_all x1, waiting for transfers between devices, spectrum(): lax.all_to_all(signal.reshape(ctx_count, row_count, columns), 'ctx', spli...  48.1 us
    all_to_all x3, local copies, waits for them, and re-layouts, to_signal(): lax.all_to_all(jnp.concatenate([turned_real, turned_imag], axis=2), 'ctx'...  23.4 us
    reduce_sum x1, other arithmetic, filter_terms(): filt_real = jnp.sum(weight * geo_real, axis=0)  23 us
  transfers between devices with their start and end apart: 4, of which 3 were waited for; matrix products, arithmetic and copies ran while one was open for 0% of the time, Pallas kernels for 0%

commit v1 on v0

v1 whole, which is shorter than its diff:
```python
import functools

import jax
import jax.numpy as jnp
from jax import lax
from jax.experimental import pallas as pl
from jax.experimental.pallas import tpu as pltpu
from jax.sharding import PartitionSpec as P

SUB = 8
LANES = 128
MESH = pl.DeviceIdType.MESH
F32 = jnp.float32


def one_minus_exp(u):
    total = jnp.ones_like(u)
    for order in range(8, 1, -1):
        total = 1.0 - (u / order) * total
    return u * total


def columns_of(block):
    return pl.ds(pl.multiple_of(block * LANES, LANES), LANES)


def kernel(
    n_ctx, n_seq, query, key, value, cot, res_ref, rate_ref,
    out, grad_query, grad_key, grad_value, grad_res,
    query_p, key_p, value_p, cot_p, mix_p, adj_p, conv_p, back_p, before, after,
    lam_row, lam16_row, weight_row, rate_tile, scale_tile,
    state_out, state_in, carry_out, carry_in, lag_out, lag_in, part_in, grad_all,
    state_send, state_recv, carry_send, carry_recv, lag_send, lag_recv,
    part_send, part_recv, grad_send, grad_recv,
):
    me = lax.axis_index("ctx")
    my_seq = lax.axis_index("seq")
    length, channels = query.shape
    modes = res_ref.shape[0]
    steps = length // SUB
    n_blocks = channels // LANES
    halves = modes // SUB
    n_tiles = n_blocks * halves
    per_owner = n_tiles // n_ctx
    owners_per_group = max(1, halves // per_owner)
    blocks_per_group = max(1, per_owner // halves)
    n_groups = n_ctx // owners_per_group
    my_group = me // owners_per_group

    def peer(distance):
        return lax.rem(me + distance, n_ctx)

    def seq_peer(distance):
        return lax.rem(my_seq + distance, n_seq)

    def remote(src, dst, send, recv, target):
        return pltpu.make_async_remote_copy(
            src_ref=src, dst_ref=dst, send_sem=send, recv_sem=recv,
            device_id=target, device_id_type=MESH,
        )

    def owned(ref, owner):
        return ref.at[pl.ds(owner * per_owner, per_owner)]

    def state_copy(owner, slot):
        return remote(owned(state_out, owner), state_in.at[slot], state_send.at[owner], state_recv.at[slot], {"ctx": owner})

    def lag_copy(owner, slot):
        return remote(owned(lag_out, owner), lag_in.at[slot], lag_send.at[owner], lag_recv.at[slot], {"ctx": owner})

    def carry_copy(target, slot):
        return remote(carry_out.at[target], owned(carry_in, slot), carry_send.at[target], carry_recv.at[slot], {"ctx": target})

    def part_copy(target, slot):
        return remote(part_in.at[my_seq], part_in.at[slot], part_send.at[target], part_recv.at[slot], {"seq": target})

    def grad_copy(target, slot):
        return remote(owned(grad_all, me), owned(grad_all, slot), grad_send.at[target], grad_recv.at[slot], {"ctx": target})

    barrier = pltpu.get_barrier_semaphore()
    for distance in range(1, n_ctx):
        pl.semaphore_signal(barrier, inc=1, device_id={"ctx": peer(distance)}, device_id_type=MESH)
    for distance in range(1, n_seq):
        pl.semaphore_signal(barrier, inc=1, device_id={"seq": seq_peer(distance)}, device_id_type=MESH)

    for block in range(n_blocks):
        cols = slice(block * LANES, (block + 1) * LANES)
        rate = rate_ref[:, cols]
        scale = jnp.sqrt(one_minus_exp(2.0 * rate))
        lam_row[block] = jnp.exp(-rate)
        lam16_row[block] = jnp.exp(-float(steps) * rate)
        weight_row[block] = res_ref[:, cols] * scale
        for half in range(halves):
            rows = slice(half * SUB, (half + 1) * SUB)
            rate_tile[block * halves + half] = rate[rows]
            scale_tile[block * halves + half] = scale[rows]

    row = lax.broadcasted_iota(jnp.int32, (length, length), 0)
    col = lax.broadcasted_iota(jnp.int32, (length, length), 1)
    to_steps = jnp.where(col == steps * (row % SUB) + row // SUB, 1.0, 0.0).astype(jnp.bfloat16)
    to_tokens = jnp.where(row == steps * (col % SUB) + col // SUB, 1.0, 0.0).astype(jnp.bfloat16)
    sub = lax.broadcasted_iota(jnp.int32, (SUB, LANES), 0)
    sub_f = sub.astype(F32)

    def wide(ref, block, mode):
        return jnp.broadcast_to(ref[block, pl.ds(mode, 1), :], (SUB, LANES))

    def cut(array):
        return [array[step * SUB:(step + 1) * SUB] for step in range(steps)]

    def states_of(block):
        cols = columns_of(block)

        def turned(ref):
            return jnp.dot(to_steps, ref[:, cols], preferred_element_type=F32)

        key_here, value_here, query_here, cot_here = turned(key), turned(value), turned(query), turned(cot)
        query_p[block], key_p[block], value_p[block], cot_p[block] = query_here, key_here, value_here, cot_here
        mixed = key_here * value_here
        adjoint = cot_here * query_here
        mix_p[block] = mixed
        adj_p[block] = adjoint
        mix, adj = cut(mixed), cut(adjoint)
        for mode in range(modes):
            tile, place = block * halves + mode // SUB, mode % SUB
            lam = wide(lam_row, block, mode)
            lam16 = wide(lam16_row, block, mode)
            last = mix[0]
            first = adj[-1]
            for step in range(1, steps):
                last = last * lam + mix[step]
                first = first * lam + adj[steps - 1 - step]
            up, down, power = last, first, lam16
            for shift in (1, 2, 4):
                up = up + jnp.where(sub >= shift, power, 0.0) * pltpu.roll(up, shift, 0)
                down = down + jnp.where(sub < SUB - shift, power, 0.0) * pltpu.roll(down, SUB - shift, 0)
                power = power * power
            ahead = jnp.where(sub >= 1, pltpu.roll(up, 1, 0), 0.0)
            before[block, mode] = ahead
            after[block, mode] = jnp.where(sub < SUB - 1, pltpu.roll(down, SUB - 1, 0), 0.0)
            state_out[tile, 0, pl.ds(place, 1), :] = up[SUB - 1:SUB]
            state_out[tile, 1, pl.ds(place, 1), :] = down[0:1]
            lag_out[tile, pl.ds(place, 1), :] = jnp.sum(first * ahead, axis=0, keepdims=True)

    def first_pass(index, _):
        group = lax.rem(my_group + index, n_groups)

        def one(inner, _):
            states_of(group * blocks_per_group + inner)
            return 0

        lax.fori_loop(0, blocks_per_group, one, 0)

        @pl.when(index == 1)
        def _():
            pl.semaphore_wait(barrier, n_ctx - 1 + n_seq - 1)

        for inner in range(owners_per_group):
            owner = group * owners_per_group + inner

            @pl.when(owner != me)
            def _():
                state_copy(owner, me).start()

            @pl.when(owner == me)
            def _():
                state_in[me] = state_out[pl.ds(me * per_owner, per_owner)]

        return 0

    lax.fori_loop(1, n_groups + 1, first_pass, 0)

    def chunk_terms(block):
        mix = cut(mix_p[block])
        adj = cut(adj_p[block])
        lam = [lam_row[block, pl.ds(half * SUB, SUB), :] for half in range(halves)]
        power = [weight_row[block, pl.ds(half * SUB, SUB), :] for half in range(halves)]
        taps = []
        for step in range(steps):
            taps.append(jnp.broadcast_to(jnp.sum(sum(power), axis=0, keepdims=True), (SUB, LANES)))
            power = [left * right for left, right in zip(power, lam)]
        for step in range(steps):
            total = taps[0] * mix[step]
            for other in range(step):
                total = total + taps[step - other] * mix[other]
            conv_p[block, pl.ds(step * SUB, SUB), :] = total
            total = taps[0] * adj[step]
            for other in range(step + 1, steps):
                total = total + taps[other - step] * adj[other]
            back_p[block, pl.ds(step * SUB, SUB), :] = total
        sums = [None] * halves
        for lag in range(steps - 1, -1, -1):
            total = adj[lag] * mix[0]
            for step in range(lag + 1, steps):
                total = total + adj[step] * mix[step - lag]
            level = jnp.broadcast_to(jnp.sum(total, axis=0, keepdims=True), (SUB, LANES))
            sums = [level if have is None else have * left + level for have, left in zip(sums, lam)]
        for half in range(halves):
            tile = block * halves + half
            lag_out[tile] = sums[half] + lam[half] * lag_out[tile]

    def second_pass(index, _):
        group = lax.rem(my_group + index, n_groups)

        def one(inner, _):
            chunk_terms(group * blocks_per_group + inner)
            return 0

        lax.fori_loop(0, blocks_per_group, one, 0)
        for inner in range(owners_per_group):
            owner = group * owners_per_group + inner

            @pl.when(owner != me)
            def _():
                lag_copy(owner, me).start()

            @pl.when(owner == me)
            def _():
                lag_in[me] = lag_out[pl.ds(me * per_owner, per_owner)]

        return 0

    lax.fori_loop(1, n_groups + 1, second_pass, 0)

    for distance in range(1, n_ctx):
        source = peer(n_ctx - distance)
        state_copy(source, source).wait_recv()
    for place in range(per_owner):
        rate = rate_tile[me * per_owner + place]
        lam = jnp.exp(-rate)
        hop = jnp.exp(-float(length) * rate)
        carried = jnp.zeros((SUB, LANES), F32)
        cross = jnp.zeros((SUB, LANES), F32)
        for source in range(n_ctx):
            carry_out[source, place, 0] = carried
            cross = cross + carried * state_in[source, place, 1]
            carried = carried * hop + state_in[source, place, 0]
        part_in[my_seq, place] = lam * cross
        carried = jnp.zeros((SUB, LANES), F32)
        for source in range(n_ctx - 1, -1, -1):
            carry_out[source, place, 1] = carried
            carried = carried * hop + state_in[source, place, 1]
    for distance in range(1, n_ctx):
        carry_copy(peer(distance), me).start()
    carry_in[pl.ds(me * per_owner, per_owner)] = carry_out[me]

    for distance in range(1, n_ctx):
        source = peer(n_ctx - distance)
        lag_copy(source, source).wait_recv()
    for place in range(per_owner):
        total = part_in[my_seq, place]
        for source in range(n_ctx):
            total = total + lag_in[source, place]
        part_in[my_seq, place] = total * scale_tile[me * per_owner + place]
    for distance in range(1, n_seq):
        part_copy(seq_peer(distance), my_seq).start()

    def finish(block):
        cols = columns_of(block)
        conv = cut(conv_p[block])
        back = cut(back_p[block])
        for mode in range(modes):
            tile, place = block * halves + mode // SUB, mode % SUB
            lam = wide(lam_row, block, mode)
            lead = lam * wide(weight_row, block, mode)
            rate = jnp.broadcast_to(rate_tile[tile, pl.ds(place, 1), :], (SUB, LANES)) * float(steps)
            carried = jnp.broadcast_to(carry_in[tile, 0, pl.ds(place, 1), :], (SUB, LANES))
            term = lead * (before[block, mode] + jnp.exp(-sub_f * rate) * carried)
            carried = jnp.broadcast_to(carry_in[tile, 1, pl.ds(place, 1), :], (SUB, LANES))
            other = lead * (after[block, mode] + jnp.exp((sub_f - (SUB - 1.0)) * rate) * carried)
            for step in range(steps):
                conv[step] = conv[step] + term
                back[steps - 1 - step] = back[steps - 1 - step] + other
                if step + 1 < steps:
                    term = term * lam
                    other = other * lam
        conv = jnp.concatenate(conv, axis=0)
        back = jnp.concatenate(back, axis=0)

        def put(ref, wide_result):
            rounded = wide_result.astype(jnp.bfloat16)
            ref[:, cols] = jnp.dot(to_tokens, rounded, preferred_element_type=F32).astype(jnp.bfloat16)

        put(out, query_p[block] * conv)
        put(grad_query, cot_p[block] * conv)
        put(grad_key, value_p[block] * back)
        put(grad_value, key_p[block] * back)

    def last_pass(index, _):
        group = lax.rem(my_group + n_groups - index, n_groups)
        for inner in range(owners_per_group):
            owner = group * owners_per_group + inner

            @pl.when(owner != me)
            def _():
                carry_copy(owner, owner).wait_recv()

        def one(inner, _):
            finish(group * blocks_per_group + inner)
            return 0

        lax.fori_loop(0, blocks_per_group, one, 0)

        @pl.when(index == n_groups // 2)
        def _():
            for distance in range(1, n_seq):
                source = seq_peer(n_seq - distance)
                part_copy(source, source).wait_recv()
            for place in range(per_owner):
                total = part_in[0, place]
                for source in range(1, n_seq):
                    total = total + part_in[source, place]
                grad_all[me * per_owner + place] = total * (1.0 / (length * n_ctx * n_seq))
            for distance in range(1, n_ctx):
                grad_copy(peer(distance), me).start()

        return 0

    lax.fori_loop(0, n_groups, last_pass, 0)

    for distance in range(1, n_ctx):
        source = peer(n_ctx - distance)
        grad_copy(source, source).wait_recv()
    for block in range(n_blocks):
        for half in range(halves):
            grad_res[half * SUB:(half + 1) * SUB, block * LANES:(block + 1) * LANES] = grad_all[block * halves + half]

    for distance in range(1, n_ctx):
        target = peer(distance)
        state_copy(target, me).wait_send()
        lag_copy(target, me).wait_send()
        carry_copy(target, me).wait_send()
        grad_copy(target, me).wait_send()
    for distance in range(1, n_seq):
        part_copy(seq_peer(distance), my_seq).wait_send()


def on_device(n_ctx, n_seq, query_input, key_input, value_input, cotangent, residues, decay_rates):
    _, length, channels = query_input.shape
    modes = residues.shape[1]
    n_blocks = channels // LANES
    halves = modes // SUB
    n_tiles = n_blocks * halves
    per_owner = n_tiles // n_ctx

    def rows():
        return pltpu.VMEM((n_blocks, length, LANES), F32)

    def tiles(*leading):
        return pltpu.VMEM(leading + (SUB, LANES), F32)

    signal = jax.ShapeDtypeStruct((length, channels), jnp.bfloat16)
    vmem = pl.BlockSpec(memory_space=pltpu.VMEM)
    results = pl.pallas_call(
        functools.partial(kernel, n_ctx, n_seq),
        out_shape=[signal] * 4 + [jax.ShapeDtypeStruct((modes, channels), F32)],
        in_specs=[vmem] * 6,
        out_specs=[vmem] * 5,
        scratch_shapes=[rows() for _ in range(8)]
        + [tiles(n_blocks, modes), tiles(n_blocks, modes)]
        + [pltpu.VMEM((n_blocks, modes, LANES), F32) for _ in range(3)]
        + [tiles(n_tiles), tiles(n_tiles)]
        + [
            tiles(n_tiles, 2), tiles(n_ctx, per_owner, 2),
            tiles(n_ctx, per_owner, 2), tiles(n_tiles, 2),
            tiles(n_tiles), tiles(n_ctx, per_owner),
            tiles(n_seq, per_owner), tiles(n_tiles),
        ]
        + [pltpu.SemaphoreType.DMA((n_ctx,)) for _ in range(6)]
        + [pltpu.SemaphoreType.DMA((n_seq,)) for _ in range(2)]
        + [pltpu.SemaphoreType.DMA((n_ctx,)) for _ in range(2)],
        compiler_params=pltpu.CompilerParams(
            collective_id=0, has_side_effects=True, vmem_limit_bytes=48 * 1024 * 1024
        ),
        cost_estimate=pl.CostEstimate(flops=100_000_000, bytes_accessed=4_500_000, transcendentals=1_000_000),
        name="modal_states",
    )(query_input[0], key_input[0], value_input[0], cotangent[0], residues.T, decay_rates.T)
    return tuple(array[None] for array in results[:4]) + (results[4].T,)


def solution(mesh):
    wide = P("seq", "ctx", None)
    return jax.shard_map(
        functools.partial(on_device, mesh.shape["ctx"], mesh.shape["seq"]),
        mesh=mesh,
        in_specs=(wide, wide, wide, wide, P(), P()),
        out_specs=(wide, wide, wide, wide, P()),
        check_vma=False,
    )
```

time: 794 us -> 39.5 us (0.05)
  waiting for transfers between devices: 373 us -> 0 us
  blocking collectives: 187 us -> 0 us
  matrix products: 75.1 us -> 0 us
  other arithmetic: 58.2 us -> 0 us
  local copies, waits for them, and re-layouts: 63.4 us -> 9.79 us
  Pallas kernels: 0 us -> 28.7 us
  starting transfers between devices: 16.4 us -> 0 us
  between operations: 14.6 us -> 0.66 us
    all_to_all x3 -> x0, waiting for transfers between devices: 229 us -> none  [the longest x1 181 us: spectrum(): lax.all_to_all(jnp.concatenate([turned_real, turned_imag], axis=2), 'ctx'...]
    all_to_all x1 -> x0, blocking collectives: 187 us -> none  [to_signal(): lax.all_to_all(jnp.concatenate([turned_real, turned_imag], axis=2), 'ctx'...]
    psum x1 -> x0, waiting for transfers between devices: 144 us -> none  [on_device(): summed = lax.psum(filter_part, ('ctx', 'seq'))]
    dot_general x8 -> x0, matrix products: 75.1 us -> none  [the longest x4 55.5 us: complex_apply(): product = jnp.einsum(joined, table, stacked, precision=HIGH)]
    pallas_call x0 -> x1, Pallas kernels: none -> 28.7 us  [on_device(): pl.pallas_call(functools.partial(kernel, n_ctx, n_seq), out_shape=[signal...]
    all_to_all x4 -> x0, local copies, waits for them, and re-layouts: 27.4 us -> none  [the longest x3 23.4 us: to_signal(): lax.all_to_all(jnp.concatenate([turned_real, turned_imag], axis=2), 'ctx'...]
    reduce_sum x1 -> x0, other arithmetic: 23 us -> none  [filter_terms(): filt_real = jnp.sum(weight * geo_real, axis=0)]
    all_to_all x3 -> x0, starting transfers between devices: 16.4 us -> none  [the longest x1 7.28 us: spectrum(): lax.all_to_all(signal.reshape(ctx_count, row_count, columns), 'ctx', spli...]
  transfers between devices with their start and end apart: 4 -> 0, of which waited for: 3 -> 0; matrix products, arithmetic and copies ran while one was open for 0% -> 0% of each run, Pallas kernels for 0% -> 0%
where the time goes in v1:
time: 39.5 us; the launch traced here: 39.1 us
  Pallas kernels  28.7 us (73%)
  local copies, waits for them, and re-layouts  9.79 us (25%)
  between operations  0.66 us (2%)
    pallas_call x1, Pallas kernels, on_device(): pl.pallas_call(functools.partial(kernel, n_ctx, n_seq), out_shape=[signal...  28.7 us
    unnamed x17, local copies, waits for them, and re-layouts  9.79 us

profile of v1, /device:TPU:0, one launch (start us, length us, event | category | flops | bytes accessed | tf_op | source)
XLA Modules:
  0.0 39.1 jit_solution(11710185472897496351)
XLA Ops:
  0.6 0.0 copy-start
  0.6 1.0 %copy-done = bf16[1,128,2048]{2,1,0:T(8,128)(2,1)S(1)} copy-done((bf16[1,128,2048]{2,1,0:T(8,128)(2,1)S(1)}, bf16[1,128,2048]{2,1,0:T(8,128)(2,1)}, u32[]{:S(2)}) %copy-start) | copy-done | bytes 524312
  1.7 0.0 copy-start.1
  1.7 1.0 %copy-done.1 = bf16[1,128,2048]{2,1,0:T(8,128)(2,1)S(1)} copy-done((bf16[1,128,2048]{2,1,0:T(8,128)(2,1)S(1)}, bf16[1,128,2048]{2,1,0:T(8,128)(2,1)}, u32[]{:S(2)}) %copy-start.1) | copy-done | bytes 524312
  2.7 0.0 copy-start.2
  2.7 1.0 %copy-done.2 = bf16[1,128,2048]{2,1,0:T(8,128)(2,1)S(1)} copy-done((bf16[1,128,2048]{2,1,0:T(8,128)(2,1)S(1)}, bf16[1,128,2048]{2,1,0:T(8,128)(2,1)}, u32[]{:S(2)}) %copy-start.2) | copy-done | bytes 524312
  3.8 0.0 copy-start.3
  3.8 1.0 %copy-done.3 = bf16[1,128,2048]{2,1,0:T(8,128)(2,1)S(1)} copy-done((bf16[1,128,2048]{2,1,0:T(8,128)(2,1)S(1)}, bf16[1,128,2048]{2,1,0:T(8,128)(2,1)}, u32[]{:S(2)}) %copy-start.3) | copy-done | bytes 524312
  4.8 0.0 copy-start.4
  4.8 0.9 %copy-done.4 = f32[2048,16]{0,1:T(8,128)S(1)} copy-done((f32[2048,16]{0,1:T(8,128)S(1)}, f32[2048,16]{0,1:T(8,128)}, u32[]{:S(2)}) %copy-start.4) | copy-done | bytes 131096
  5.7 0.0 copy-start.5
  5.7 0.9 %copy-done.5 = f32[2048,16]{0,1:T(8,128)S(1)} copy-done((f32[2048,16]{0,1:T(8,128)S(1)}, f32[2048,16]{0,1:T(8,128)}, u32[]{:S(2)}) %copy-start.5) | copy-done | bytes 131096
  6.6 28.7 %modal_states.1 = (bf16[128,2048]{1,0:T(8,128)(2,1)S(1)}, bf16[128,2048]{1,0:T(8,128)(2,1)S(1)}, bf16[128,2048]{1,0:T(8,128)(2,1)S(1)}, bf16[128,2048]{1,0:T(8,128)(2,1)S(1)}, f32[16,2048]{1,0:T(8,128)S(1)}) custom-call(bf16[128,2048]{1,0:T(8,128)(2,1)S(1)} %bitcast.15, bf16[128,2048]{1,0:T(8,128)(2,1)S(1)} %bitcast.16, bf16[128,2048]{1,0:T(8,128)(2,1)S(1)} %bitcast.17, ...), custom_call_target="tpu_custom_call" | custom-call | flops 100000000 | bytes 4500000 | tf_op jit(solution)/shard_map/modal_states/pallas_call | solution.py:354
  35.3 0.8 %copy.16 = bf16[1,128,2048]{2,1,0:T(8,128)(2,1)} copy(bf16[1,128,2048]{2,1,0:T(8,128)(2,1)S(1)} %bitcast.14) | data formatting | bytes 1048576
  36.1 0.8 %copy.17 = bf16[1,128,2048]{2,1,0:T(8,128)(2,1)} copy(bf16[1,128,2048]{2,1,0:T(8,128)(2,1)S(1)} %bitcast.13) | data formatting | bytes 1048576
  36.9 0.8 %copy.18 = bf16[1,128,2048]{2,1,0:T(8,128)(2,1)} copy(bf16[1,128,2048]{2,1,0:T(8,128)(2,1)S(1)} %bitcast.12) | data formatting | bytes 1048576
  37.7 0.8 %copy.19 = bf16[1,128,2048]{2,1,0:T(8,128)(2,1)} copy(bf16[1,128,2048]{2,1,0:T(8,128)(2,1)S(1)} %bitcast.11) | data formatting | bytes 1048576
  38.5 0.7 %copy.20 = f32[2048,16]{0,1:T(8,128)} copy(f32[2048,16]{0,1:T(8,128)S(1)} %bitcast.21) | data formatting | bytes 262144
Async XLA Ops:
  0.6 1.0 %copy-start = (bf16[1,128,2048]{2,1,0:T(8,128)(2,1)S(1)}, bf16[1,128,2048]{2,1,0:T(8,128)(2,1)}, u32[]{:S(2)}) copy-start(bf16[1,128,2048]{2,1,0:T(8,128)(2,1)} %param.6) | copy-start | bytes 1572868
  1.7 1.0 %copy-start.1 = (bf16[1,128,2048]{2,1,0:T(8,128)(2,1)S(1)}, bf16[1,128,2048]{2,1,0:T(8,128)(2,1)}, u32[]{:S(2)}) copy-start(bf16[1,128,2048]{2,1,0:T(8,128)(2,1)} %param.7) | copy-start | bytes 1572868
  2.7 1.0 %copy-start.2 = (bf16[1,128,2048]{2,1,0:T(8,128)(2,1)S(1)}, bf16[1,128,2048]{2,1,0:T(8,128)(2,1)}, u32[]{:S(2)}) copy-start(bf16[1,128,2048]{2,1,0:T(8,128)(2,1)} %param.8) | copy-start | bytes 1572868
  3.8 1.0 %copy-start.3 = (bf16[1,128,2048]{2,1,0:T(8,128)(2,1)S(1)}, bf16[1,128,2048]{2,1,0:T(8,128)(2,1)}, u32[]{:S(2)}) copy-start(bf16[1,128,2048]{2,1,0:T(8,128)(2,1)} %param.9) | copy-start | bytes 1572868
  4.8 0.9 %copy-start.4 = (f32[2048,16]{0,1:T(8,128)S(1)}, f32[2048,16]{0,1:T(8,128)}, u32[]{:S(2)}) copy-start(f32[2048,16]{0,1:T(8,128)} %param.10) | copy-start | bytes 393220
  5.7 0.9 %copy-start.5 = (f32[2048,16]{0,1:T(8,128)S(1)}, f32[2048,16]{0,1:T(8,128)}, u32[]{:S(2)}) copy-start(f32[2048,16]{0,1:T(8,128)} %param.11) | copy-start | bytes 393220

commit v2 on v1

--- a/solution.py
+++ b/solution.py
@@ -24,14 +24,23 @@
     return pl.ds(pl.multiple_of(block * LANES, LANES), LANES)
 
 
+def step_order(length, steps, inverse):
+    row = lax.broadcasted_iota(jnp.int32, (length, length), 0)
+    col = lax.broadcasted_iota(jnp.int32, (length, length), 1)
+    if inverse:
+        row, col = col, row
+    return jnp.where(col == steps * (row % SUB) + row // SUB, 1.0, 0.0).astype(jnp.bfloat16)
+
+
 def kernel(
-    n_ctx, n_seq, query, key, value, cot, res_ref, rate_ref,
+    n_ctx, n_seq, n_parts, query_hbm, key_hbm, value_hbm, cot_hbm, res_hbm, rate_hbm,
     out, grad_query, grad_key, grad_value, grad_res,
-    query_p, key_p, value_p, cot_p, mix_p, adj_p, conv_p, back_p, before, after,
+    query, key, value, cot, res_ref, rate_ref,
+    query_p, key_p, value_p, cot_p, mix_p, adj_p, conv_p, back_p, before, after, up_turn, down_turn,
     lam_row, lam16_row, weight_row, rate_tile, scale_tile,
     state_out, state_in, carry_out, carry_in, lag_out, lag_in, part_in, grad_all,
     state_send, state_recv, carry_send, carry_recv, lag_send, lag_recv,
-    part_send, part_recv, grad_send, grad_recv,
+    part_send, part_recv, grad_send, grad_recv, load_sem, param_sem,
 ):
     me = lax.axis_index("ctx")
     my_seq = lax.axis_index("seq")
@@ -46,6 +55,21 @@
     blocks_per_group = max(1, per_owner // halves)
     n_groups = n_ctx // owners_per_group
     my_group = me // owners_per_group
+    part = channels // n_parts
+
+    def load(index, place):
+        cols = pl.ds(pl.multiple_of(place * part, LANES), part)
+        source = (key_hbm, value_hbm, query_hbm, cot_hbm)[index]
+        target = (key, value, query, cot)[index]
+        return pltpu.make_async_copy(source.at[:, cols], target.at[:, cols], load_sem.at[index, place])
+
+    rate_load = pltpu.make_async_copy(rate_hbm, rate_ref, param_sem.at[0])
+    res_load = pltpu.make_async_copy(res_hbm, res_ref, param_sem.at[1])
+    rate_load.start()
+    res_load.start()
+    for place in range(n_parts):
+        for index in range(4):
+            load(index, place).start()
 
     def peer(distance):
         return lax.rem(me + distance, n_ctx)
@@ -83,6 +107,8 @@
     for distance in range(1, n_seq):
         pl.semaphore_signal(barrier, inc=1, device_id={"seq": seq_peer(distance)}, device_id_type=MESH)
 
+    rate_load.wait()
+    res_load.wait()
     for block in range(n_blocks):
         cols = slice(block * LANES, (block + 1) * LANES)
         rate = rate_ref[:, cols]
@@ -95,61 +121,73 @@
             rate_tile[block * halves + half] = rate[rows]
             scale_tile[block * halves + half] = scale[rows]
 
-    row = lax.broadcasted_iota(jnp.int32, (length, length), 0)
-    col = lax.broadcasted_iota(jnp.int32, (length, length), 1)
-    to_steps = jnp.where(col == steps * (row % SUB) + row // SUB, 1.0, 0.0).astype(jnp.bfloat16)
-    to_tokens = jnp.where(row == steps * (col % SUB) + col // SUB, 1.0, 0.0).astype(jnp.bfloat16)
-    sub = lax.broadcasted_iota(jnp.int32, (SUB, LANES), 0)
-    sub_f = sub.astype(F32)
+    to_steps = step_order(length, steps, False)
+
+    def turn(place, _):
+        cols = pl.ds(pl.multiple_of(place * part, LANES), part)
+        for index in range(4):
+            load(index, place).wait()
+        key_here, value_here, query_here, cot_here = [
+            jnp.dot(to_steps, ref[:, cols], preferred_element_type=F32) for ref in (key, value, query, cot)
+        ]
+        mixed = key_here * value_here
+        adjoint = cot_here * query_here
+        for inner in range(part // LANES):
+            block = place * (part // LANES) + inner
+            lanes = slice(inner * LANES, (inner + 1) * LANES)
+            query_p[block] = query_here[:, lanes]
+            key_p[block] = key_here[:, lanes]
+            value_p[block] = value_here[:, lanes]
+            cot_p[block] = cot_here[:, lanes]
+            mix_p[block] = mixed[:, lanes]
+            adj_p[block] = adjoint[:, lanes]
+        return 0
+
+    lax.fori_loop(0, n_parts, turn, 0)
 
     def wide(ref, block, mode):
         return jnp.broadcast_to(ref[block, pl.ds(mode, 1), :], (SUB, LANES))
 
+    def half_rows(ref, block, half):
+        return ref[block, half * SUB:(half + 1) * SUB, :]
+
     def cut(array):
         return [array[step * SUB:(step + 1) * SUB] for step in range(steps)]
 
-    def states_of(block):
-        cols = columns_of(block)
-
-        def turned(ref):
-            return jnp.dot(to_steps, ref[:, cols], preferred_element_type=F32)
-
-        key_here, value_here, query_here, cot_here = turned(key), turned(value), turned(query), turned(cot)
-        query_p[block], key_p[block], value_p[block], cot_p[block] = query_here, key_here, value_here, cot_here
-        mixed = key_here * value_here
-        adjoint = cot_here * query_here
-        mix_p[block] = mixed
-        adj_p[block] = adjoint
-        mix, adj = cut(mixed), cut(adjoint)
+    def states_of(block, inner):
+        mix, adj = cut(mix_p[block]), cut(adj_p[block])
         for mode in range(modes):
-            tile, place = block * halves + mode // SUB, mode % SUB
             lam = wide(lam_row, block, mode)
-            lam16 = wide(lam16_row, block, mode)
             last = mix[0]
             first = adj[-1]
             for step in range(1, steps):
                 last = last * lam + mix[step]
                 first = first * lam + adj[steps - 1 - step]
-            up, down, power = last, first, lam16
-            for shift in (1, 2, 4):
-                up = up + jnp.where(sub >= shift, power, 0.0) * pltpu.roll(up, shift, 0)
-                down = down + jnp.where(sub < SUB - shift, power, 0.0) * pltpu.roll(down, SUB - shift, 0)
-                power = power * power
-            ahead = jnp.where(sub >= 1, pltpu.roll(up, 1, 0), 0.0)
-            before[block, mode] = ahead
-            after[block, mode] = jnp.where(sub < SUB - 1, pltpu.roll(down, SUB - 1, 0), 0.0)
-            state_out[tile, 0, pl.ds(place, 1), :] = up[SUB - 1:SUB]
-            state_out[tile, 1, pl.ds(place, 1), :] = down[0:1]
-            lag_out[tile, pl.ds(place, 1), :] = jnp.sum(first * ahead, axis=0, keepdims=True)
+            up_turn[inner, mode // SUB, mode % SUB] = last
+            down_turn[inner, mode // SUB, mode % SUB] = first
+        for half in range(halves):
+            tile = block * halves + half
+            lam16 = half_rows(lam16_row, block, half)
+            lasts = [up_turn[inner, half, :, chunk, :] for chunk in range(SUB)]
+            firsts = [down_turn[inner, half, :, chunk, :] for chunk in range(SUB)]
+            state = lasts[0]
+            lag = jnp.zeros_like(state)
+            for chunk in range(1, SUB):
+                before[tile, chunk] = state
+                lag = lag + firsts[chunk] * state
+                state = state * lam16 + lasts[chunk]
+            state_out[tile, 0] = state
+            lag_out[tile] = lag
+            state = firsts[-1]
+            for chunk in range(SUB - 2, -1, -1):
+                after[tile, chunk] = state
+                state = state * lam16 + firsts[chunk]
+            state_out[tile, 1] = state
 
     def first_pass(index, _):
         group = lax.rem(my_group + index, n_groups)
-
-        def one(inner, _):
-            states_of(group * blocks_per_group + inner)
-            return 0
-
-        lax.fori_loop(0, blocks_per_group, one, 0)
+        for inner in range(blocks_per_group):
+            states_of(group * blocks_per_group + inner, inner)
 
         @pl.when(index == 1)
         def _():
@@ -201,12 +239,8 @@
 
     def second_pass(index, _):
         group = lax.rem(my_group + index, n_groups)
-
-        def one(inner, _):
+        for inner in range(blocks_per_group):
             chunk_terms(group * blocks_per_group + inner)
-            return 0
-
-        lax.fori_loop(0, blocks_per_group, one, 0)
         for inner in range(owners_per_group):
             owner = group * owners_per_group + inner
 
@@ -220,7 +254,7 @@
 
         return 0
 
-    lax.fori_loop(1, n_groups + 1, second_pass, 0)
+    lax.fori_loop(1, n_groups // 2 + 1, second_pass, 0)
 
     for distance in range(1, n_ctx):
         source = peer(n_ctx - distance)
@@ -244,30 +278,28 @@
         carry_copy(peer(distance), me).start()
     carry_in[pl.ds(me * per_owner, per_owner)] = carry_out[me]
 
-    for distance in range(1, n_ctx):
-        source = peer(n_ctx - distance)
-        lag_copy(source, source).wait_recv()
-    for place in range(per_owner):
-        total = part_in[my_seq, place]
-        for source in range(n_ctx):
-            total = total + lag_in[source, place]
-        part_in[my_seq, place] = total * scale_tile[me * per_owner + place]
-    for distance in range(1, n_seq):
-        part_copy(seq_peer(distance), my_seq).start()
-
-    def finish(block):
+    lax.fori_loop(n_groups // 2 + 1, n_groups + 1, second_pass, 0)
+
+    def finish(block, inner):
         cols = columns_of(block)
+        for half in range(halves):
+            tile = block * halves + half
+            lam16 = half_rows(lam16_row, block, half)
+            lead = half_rows(lam_row, block, half) * half_rows(weight_row, block, half)
+            state = carry_in[tile, 0]
+            for chunk in range(SUB):
+                up_turn[inner, half, chunk] = lead * (state + before[tile, chunk] if chunk else state)
+                state = state * lam16
+            state = carry_in[tile, 1]
+            for chunk in range(SUB - 1, -1, -1):
+                down_turn[inner, half, chunk] = lead * (state + after[tile, chunk] if chunk < SUB - 1 else state)
+                state = state * lam16
         conv = cut(conv_p[block])
         back = cut(back_p[block])
         for mode in range(modes):
-            tile, place = block * halves + mode // SUB, mode % SUB
             lam = wide(lam_row, block, mode)
-            lead = lam * wide(weight_row, block, mode)
-            rate = jnp.broadcast_to(rate_tile[tile, pl.ds(place, 1), :], (SUB, LANES)) * float(steps)
-            carried = jnp.broadcast_to(carry_in[tile, 0, pl.ds(place, 1), :], (SUB, LANES))
-            term = lead * (before[block, mode] + jnp.exp(-sub_f * rate) * carried)
-            carried = jnp.broadcast_to(carry_in[tile, 1, pl.ds(place, 1), :], (SUB, LANES))
-            other = lead * (after[block, mode] + jnp.exp((sub_f - (SUB - 1.0)) * rate) * carried)
+            term = up_turn[inner, mode // SUB, :, mode % SUB, :]
+            other = down_turn[inner, mode // SUB, :, mode % SUB, :]
             for step in range(steps):
                 conv[step] = conv[step] + term
                 back[steps - 1 - step] = back[steps - 1 - step] + other
@@ -276,15 +308,10 @@
                     other = other * lam
         conv = jnp.concatenate(conv, axis=0)
         back = jnp.concatenate(back, axis=0)
-
-        def put(ref, wide_result):
-            rounded = wide_result.astype(jnp.bfloat16)
-            ref[:, cols] = jnp.dot(to_tokens, rounded, preferred_element_type=F32).astype(jnp.bfloat16)
-
-        put(out, query_p[block] * conv)
-        put(grad_query, cot_p[block] * conv)
-        put(grad_key, value_p[block] * back)
-        put(grad_value, key_p[block] * back)
+        out[:, cols] = (query_p[block] * conv).astype(jnp.bfloat16)
+        grad_query[:, cols] = (cot_p[block] * conv).astype(jnp.bfloat16)
+        grad_key[:, cols] = (value_p[block] * back).astype(jnp.bfloat16)
+        grad_value[:, cols] = (key_p[block] * back).astype(jnp.bfloat16)
 
     def last_pass(index, _):
         group = lax.rem(my_group + n_groups - index, n_groups)
@@ -295,11 +322,21 @@
             def _():
                 carry_copy(owner, owner).wait_recv()
 
-        def one(inner, _):
-            finish(group * blocks_per_group + inner)
-            return 0
-
-        lax.fori_loop(0, blocks_per_group, one, 0)
+        for inner in range(blocks_per_group):
+            finish(group * blocks_per_group + inner, inner)
+
+        @pl.when(index == 0)
+        def _():
+            for distance in range(1, n_ctx):
+                source = peer(n_ctx - distance)
+                lag_copy(source, source).wait_recv()
+            for place in range(per_owner):
+                total = part_in[my_seq, place]
+                for source in range(n_ctx):
+                    total = total + lag_in[source, place]
+                part_in[my_seq, place] = total * scale_tile[me * per_owner + place]
+            for distance in range(1, n_seq):
+                part_copy(seq_peer(distance), my_seq).start()
 
         @pl.when(index == n_groups // 2)
         def _():
@@ -335,6 +372,28 @@
         part_copy(seq_peer(distance), my_seq).wait_send()
 
 
+def writer(out_p, grad_query_p, grad_key_p, grad_value_p, grad_res, out, grad_query, grad_key, grad_value, grad_res_hbm, *scratch):
+    stage, sems, grad_sem = scratch[:4], scratch[4], scratch[5]
+    length, channels = out_p.shape
+    n_parts = sems.shape[1]
+    part = channels // n_parts
+    whole = pltpu.make_async_copy(grad_res, grad_res_hbm, grad_sem)
+    whole.start()
+    to_tokens = step_order(length, length // SUB, True)
+    copies = []
+    for place in range(n_parts):
+        cols = slice(place * part, (place + 1) * part)
+        for index, (source, target) in enumerate(
+            zip((out_p, grad_query_p, grad_key_p, grad_value_p), (out, grad_query, grad_key, grad_value))
+        ):
+            stage[index][:, cols] = jnp.dot(to_tokens, source[:, cols], preferred_element_type=F32).astype(jnp.bfloat16)
+            copies.append(pltpu.make_async_copy(stage[index].at[:, cols], target.at[:, cols], sems.at[index, place]))
+            copies[-1].start()
+    for copy in copies:
+        copy.wait()
+    whole.wait()
+
+
 def on_device(n_ctx, n_seq, query_input, key_input, value_input, cotangent, residues, decay_rates):
     _, length, channels = query_input.shape
     modes = residues.shape[1]
@@ -351,13 +410,19 @@
 
     signal = jax.ShapeDtypeStruct((length, channels), jnp.bfloat16)
     vmem = pl.BlockSpec(memory_space=pltpu.VMEM)
+    hbm = pl.BlockSpec(memory_space=pltpu.HBM)
+    n_parts = 4
+    wide_rows = [pltpu.VMEM((length, channels), jnp.bfloat16) for _ in range(4)]
     results = pl.pallas_call(
-        functools.partial(kernel, n_ctx, n_seq),
+        functools.partial(kernel, n_ctx, n_seq, n_parts),
         out_shape=[signal] * 4 + [jax.ShapeDtypeStruct((modes, channels), F32)],
-        in_specs=[vmem] * 6,
+        in_specs=[hbm] * 6,
         out_specs=[vmem] * 5,
-        scratch_shapes=[rows() for _ in range(8)]
-        + [tiles(n_blocks, modes), tiles(n_blocks, modes)]
+        scratch_shapes=wide_rows
+        + [pltpu.VMEM((modes, channels), F32) for _ in range(2)]
+        + [rows() for _ in range(8)]
+        + [tiles(n_tiles, SUB), tiles(n_tiles, SUB)]
+        + [tiles(max(1, per_owner // halves), halves, SUB) for _ in range(2)]
         + [pltpu.VMEM((n_blocks, modes, LANES), F32) for _ in range(3)]
         + [tiles(n_tiles), tiles(n_tiles)]
         + [
@@ -368,13 +433,24 @@
         ]
         + [pltpu.SemaphoreType.DMA((n_ctx,)) for _ in range(6)]
         + [pltpu.SemaphoreType.DMA((n_seq,)) for _ in range(2)]
-        + [pltpu.SemaphoreType.DMA((n_ctx,)) for _ in range(2)],
+        + [pltpu.SemaphoreType.DMA((n_ctx,)) for _ in range(2)]
+        + [pltpu.SemaphoreType.DMA((4, n_parts)), pltpu.SemaphoreType.DMA((2,))],
         compiler_params=pltpu.CompilerParams(
-            collective_id=0, has_side_effects=True, vmem_limit_bytes=48 * 1024 * 1024
+            collective_id=0, has_side_effects=True, vmem_limit_bytes=829 * 64 * 1024
         ),
         cost_estimate=pl.CostEstimate(flops=100_000_000, bytes_accessed=4_500_000, transcendentals=1_000_000),
         name="modal_states",
     )(query_input[0], key_input[0], value_input[0], cotangent[0], residues.T, decay_rates.T)
+    results = pl.pallas_call(
+        writer,
+        out_shape=[signal] * 4 + [jax.ShapeDtypeStruct((modes, channels), F32)],
+        in_specs=[vmem] * 5,
+        out_specs=[hbm] * 5,
+        scratch_shapes=wide_rows + [pltpu.SemaphoreType.DMA((4, n_parts)), pltpu.SemaphoreType.DMA],
+        compiler_params=pltpu.CompilerParams(vmem_limit_bytes=16 * 1024 * 1024),
+        cost_estimate=pl.CostEstimate(flops=300_000_000, bytes_accessed=4_500_000, transcendentals=0),
+        name="token_order",
+    )(*results)
     return tuple(array[None] for array in results[:4]) + (results[4].T,)
 
 

time: 39.5 us -> 38.5 us (0.975)
  local copies, waits for them, and re-layouts: 9.79 us -> 2.84 us
  Pallas kernels: 28.7 us -> 34.8 us
    unnamed x17 -> x6, local copies, waits for them, and re-layouts: 9.79 us -> 2.84 us
    pallas_call x1 -> x2, Pallas kernels: 28.7 us -> 34.8 us  [the longest x1 33.1 us: on_device(): pl.pallas_call(functools.partial(kernel, n_ctx, n_seq, n_parts), out_shap...]
where the time goes in v2:
time: 38.5 us; the launch traced here: 38.3 us
  Pallas kernels  34.8 us (90%)
  local copies, waits for them, and re-layouts  2.84 us (7%)
  between operations  0.66 us (2%)
    pallas_call x1, Pallas kernels, on_device(): pl.pallas_call(functools.partial(kernel, n_ctx, n_seq, n_parts), out_shap...  33.1 us
    unnamed x6, local copies, waits for them, and re-layouts  2.84 us
    pallas_call x1, Pallas kernels, on_device(): pl.pallas_call(writer, out_shape=[signal] * 4 + [jax.ShapeDtypeStruct((mo...  1.67 us

profile of v2, /device:TPU:0, one launch (start us, length us, event | category | flops | bytes accessed | tf_op | source)
XLA Modules:
  0.0 38.3 jit_solution(15027577249132242814)
XLA Ops:
  0.6 0.0 copy-start.1
  0.6 0.9 %copy-done.1 = f32[2048,16]{0,1:T(8,128)S(1)} copy-done((f32[2048,16]{0,1:T(8,128)S(1)}, f32[2048,16]{0,1:T(8,128)}, u32[]{:S(2)}) %copy-start.1) | copy-done | bytes 131096
  1.5 0.0 copy-start.2
  1.5 0.9 %copy-done.2 = f32[2048,16]{0,1:T(8,128)S(1)} copy-done((f32[2048,16]{0,1:T(8,128)S(1)}, f32[2048,16]{0,1:T(8,128)}, u32[]{:S(2)}) %copy-start.2) | copy-done | bytes 131096
  2.4 33.1 %modal_states.1 = (bf16[128,2048]{1,0:T(8,128)(2,1)S(1)}, bf16[128,2048]{1,0:T(8,128)(2,1)S(1)}, bf16[128,2048]{1,0:T(8,128)(2,1)S(1)}, bf16[128,2048]{1,0:T(8,128)(2,1)}, f32[16,2048]{1,0:T(8,128)S(1)}) custom-call(bf16[128,2048]{1,0:T(8,128)(2,1)} %bitcast.13, bf16[128,2048]{1,0:T(8,128)(2,1)} %bitcast.14, bf16[128,2048]{1,0:T(8,128)(2,1)} %bitcast.15, ...), custom_call_target="tpu_custom_call" | custom-call | flops 100000000 | bytes 4500000 | tf_op jit(solution)/shard_map/modal_states/pallas_call | solution.py:416
  35.6 0.0 copy-start
  35.6 1.0 %copy-done = bf16[128,2048]{1,0:T(8,128)(2,1)S(1)} copy-done((bf16[128,2048]{1,0:T(8,128)(2,1)S(1)}, bf16[128,2048]{1,0:T(8,128)(2,1)}, u32[]{:S(2)}) %copy-start) | copy-done | bytes 524312
  36.6 1.7 %token_order.1 = (bf16[128,2048]{1,0:T(8,128)(2,1)}, bf16[128,2048]{1,0:T(8,128)(2,1)}, bf16[128,2048]{1,0:T(8,128)(2,1)}, bf16[128,2048]{1,0:T(8,128)(2,1)}, f32[16,2048]{1,0:T(8,128)}) custom-call(bf16[128,2048]{1,0:T(8,128)(2,1)S(1)} %get-tuple-element.15.out_p, bf16[128,2048]{1,0:T(8,128)(2,1)S(1)} %get-tuple-element.16.grad_query_p, ...), custom_call_target="tpu_custom_call" | custom-call | flops 300000000 | bytes 4500000 | tf_op jit(solution)/shard_map/token_order/pallas_call | solution.py:444
Async XLA Ops:
  0.6 0.9 %copy-start.1 = (f32[2048,16]{0,1:T(8,128)S(1)}, f32[2048,16]{0,1:T(8,128)}, u32[]{:S(2)}) copy-start(f32[2048,16]{0,1:T(8,128)} %param.10) | copy-start | bytes 393220
  1.5 0.9 %copy-start.2 = (f32[2048,16]{0,1:T(8,128)S(1)}, f32[2048,16]{0,1:T(8,128)}, u32[]{:S(2)}) copy-start(f32[2048,16]{0,1:T(8,128)} %param.11) | copy-start | bytes 393220
  35.6 1.0 %copy-start = (bf16[128,2048]{1,0:T(8,128)(2,1)S(1)}, bf16[128,2048]{1,0:T(8,128)(2,1)}, u32[]{:S(2)}) copy-start(bf16[128,2048]{1,0:T(8,128)(2,1)} %get-tuple-element.18.grad_value_p) | copy-start | bytes 1572868

commit v3 on v2

--- a/solution.py
+++ b/solution.py
@@ -34,13 +34,13 @@
 
 def kernel(
     n_ctx, n_seq, n_parts, query_hbm, key_hbm, value_hbm, cot_hbm, res_hbm, rate_hbm,
-    out, grad_query, grad_key, grad_value, grad_res,
-    query, key, value, cot, res_ref, rate_ref,
+    result_hbm, grad_all,
+    query, key, value, cot, res_ref, rate_ref, result,
     query_p, key_p, value_p, cot_p, mix_p, adj_p, conv_p, back_p, before, after, up_turn, down_turn,
     lam_row, lam16_row, weight_row, rate_tile, scale_tile,
-    state_out, state_in, carry_out, carry_in, lag_out, lag_in, part_in, grad_all,
+    state_out, state_in, carry_out, carry_in, lag_out, lag_in, part_in, grad_own,
     state_send, state_recv, carry_send, carry_recv, lag_send, lag_recv,
-    part_send, part_recv, grad_send, grad_recv, load_sem, param_sem,
+    part_send, part_recv, grad_send, grad_recv, load_sem, param_sem, store_sem, own_sem,
 ):
     me = lax.axis_index("ctx")
     my_seq = lax.axis_index("seq")
@@ -99,7 +99,7 @@
         return remote(part_in.at[my_seq], part_in.at[slot], part_send.at[target], part_recv.at[slot], {"seq": target})
 
     def grad_copy(target, slot):
-        return remote(owned(grad_all, me), owned(grad_all, slot), grad_send.at[target], grad_recv.at[slot], {"ctx": target})
+        return remote(grad_own, owned(grad_all, slot), grad_send.at[target], grad_recv.at[slot], {"ctx": target})
 
     barrier = pltpu.get_barrier_semaphore()
     for distance in range(1, n_ctx):
@@ -151,20 +151,29 @@
     def half_rows(ref, block, half):
         return ref[block, half * SUB:(half + 1) * SUB, :]
 
+    def rows_at(ref, block, step):
+        return ref[block, step * SUB:(step + 1) * SUB, :]
+
+    def tree(terms):
+        while len(terms) > 1:
+            terms = [sum(terms[place:place + 2][1:], terms[place]) for place in range(0, len(terms), 2)]
+        return terms[0]
+
     def cut(array):
         return [array[step * SUB:(step + 1) * SUB] for step in range(steps)]
 
     def states_of(block, inner):
-        mix, adj = cut(mix_p[block]), cut(adj_p[block])
-        for mode in range(modes):
-            lam = wide(lam_row, block, mode)
-            last = mix[0]
-            first = adj[-1]
+        for half in range(halves):
+            lams = [wide(lam_row, block, half * SUB + mode) for mode in range(SUB)]
+            lasts = [rows_at(mix_p, block, 0)] * SUB
+            firsts = [rows_at(adj_p, block, steps - 1)] * SUB
             for step in range(1, steps):
-                last = last * lam + mix[step]
-                first = first * lam + adj[steps - 1 - step]
-            up_turn[inner, mode // SUB, mode % SUB] = last
-            down_turn[inner, mode // SUB, mode % SUB] = first
+                mix, adj = rows_at(mix_p, block, step), rows_at(adj_p, block, steps - 1 - step)
+                lasts = [have * lam + mix for have, lam in zip(lasts, lams)]
+                firsts = [have * lam + adj for have, lam in zip(firsts, lams)]
+            for mode in range(SUB):
+                up_turn[inner, half, mode] = lasts[mode]
+                down_turn[inner, half, mode] = firsts[mode]
         for half in range(halves):
             tile = block * halves + half
             lam16 = half_rows(lam16_row, block, half)
@@ -217,22 +226,26 @@
         for step in range(steps):
             taps.append(jnp.broadcast_to(jnp.sum(sum(power), axis=0, keepdims=True), (SUB, LANES)))
             power = [left * right for left, right in zip(power, lam)]
+        totals = [taps[0] * rows for rows in mix]
+        for lag in range(1, steps):
+            for step in range(lag, steps):
+                totals[step] = totals[step] + taps[lag] * mix[step - lag]
         for step in range(steps):
-            total = taps[0] * mix[step]
-            for other in range(step):
-                total = total + taps[step - other] * mix[other]
-            conv_p[block, pl.ds(step * SUB, SUB), :] = total
-            total = taps[0] * adj[step]
-            for other in range(step + 1, steps):
-                total = total + taps[other - step] * adj[other]
-            back_p[block, pl.ds(step * SUB, SUB), :] = total
-        sums = [None] * halves
-        for lag in range(steps - 1, -1, -1):
-            total = adj[lag] * mix[0]
-            for step in range(lag + 1, steps):
-                total = total + adj[step] * mix[step - lag]
-            level = jnp.broadcast_to(jnp.sum(total, axis=0, keepdims=True), (SUB, LANES))
-            sums = [level if have is None else have * left + level for have, left in zip(sums, lam)]
+            conv_p[block, step * SUB:(step + 1) * SUB, :] = totals[step]
+        totals = [taps[0] * rows for rows in adj]
+        for lag in range(1, steps):
+            for step in range(steps - lag):
+                totals[step] = totals[step] + taps[lag] * adj[step + lag]
+        for step in range(steps):
+            back_p[block, step * SUB:(step + 1) * SUB, :] = totals[step]
+        totals = [rows * mix[0] for rows in adj]
+        for step in range(1, steps):
+            for lag in range(steps - step):
+                totals[lag] = totals[lag] + adj[step + lag] * mix[step]
+        levels = [jnp.broadcast_to(jnp.sum(total, axis=0, keepdims=True), (SUB, LANES)) for total in totals]
+        sums = [levels[-1]] * halves
+        for level in levels[-2::-1]:
+            sums = [have * left + level for have, left in zip(sums, lam)]
         for half in range(halves):
             tile = block * halves + half
             lag_out[tile] = sums[half] + lam[half] * lag_out[tile]
@@ -294,24 +307,39 @@
             for chunk in range(SUB - 1, -1, -1):
                 down_turn[inner, half, chunk] = lead * (state + after[tile, chunk] if chunk < SUB - 1 else state)
                 state = state * lam16
-        conv = cut(conv_p[block])
-        back = cut(back_p[block])
-        for mode in range(modes):
-            lam = wide(lam_row, block, mode)
-            term = up_turn[inner, mode // SUB, :, mode % SUB, :]
-            other = down_turn[inner, mode // SUB, :, mode % SUB, :]
-            for step in range(steps):
-                conv[step] = conv[step] + term
-                back[steps - 1 - step] = back[steps - 1 - step] + other
-                if step + 1 < steps:
-                    term = term * lam
-                    other = other * lam
-        conv = jnp.concatenate(conv, axis=0)
-        back = jnp.concatenate(back, axis=0)
-        out[:, cols] = (query_p[block] * conv).astype(jnp.bfloat16)
-        grad_query[:, cols] = (cot_p[block] * conv).astype(jnp.bfloat16)
-        grad_key[:, cols] = (value_p[block] * back).astype(jnp.bfloat16)
-        grad_value[:, cols] = (key_p[block] * back).astype(jnp.bfloat16)
+        lams = [wide(lam_row, block, mode) for mode in range(modes)]
+
+        def put(place, step, factor, pair):
+            rows = pl.ds(step * SUB, 2 * SUB)
+            target = slice(place * length + step * SUB, place * length + (step + 2) * SUB)
+            result[target, cols] = (factor[block, rows, :] * pair).astype(jnp.bfloat16)
+
+        terms = [up_turn[inner, mode // SUB, :, mode % SUB, :] for mode in range(modes)]
+        sums = []
+        for step in range(steps):
+            sums.append(rows_at(conv_p, block, step) + tree(terms))
+            terms = [term * lam for term, lam in zip(terms, lams)]
+            if step % 2:
+                pair = jnp.concatenate(sums, axis=0)
+                put(0, step - 1, query_p, pair)
+                put(1, step - 1, cot_p, pair)
+                sums = []
+        terms = [down_turn[inner, mode // SUB, :, mode % SUB, :] for mode in range(modes)]
+        for step in range(steps - 1, -1, -1):
+            sums.insert(0, rows_at(back_p, block, step) + tree(terms))
+            terms = [term * lam for term, lam in zip(terms, lams)]
+            if step % 2 == 0:
+                pair = jnp.concatenate(sums, axis=0)
+                put(2, step, value_p, pair)
+                put(3, step, key_p, pair)
+                sums = []
+
+    own_copy = pltpu.make_async_copy(grad_own, owned(grad_all, me), own_sem)
+
+    def store(group):
+        width = blocks_per_group * LANES
+        cols = pl.ds(pl.multiple_of(group * width, LANES), width)
+        return pltpu.make_async_copy(result.at[:, cols], result_hbm.at[:, cols], store_sem.at[group])
 
     def last_pass(index, _):
         group = lax.rem(my_group + n_groups - index, n_groups)
@@ -324,6 +352,7 @@
 
         for inner in range(blocks_per_group):
             finish(group * blocks_per_group + inner, inner)
+        store(group).start()
 
         @pl.when(index == 0)
         def _():
@@ -347,9 +376,10 @@
                 total = part_in[0, place]
                 for source in range(1, n_seq):
                     total = total + part_in[source, place]
-                grad_all[me * per_owner + place] = total * (1.0 / (length * n_ctx * n_seq))
+                grad_own[place] = total * (1.0 / (length * n_ctx * n_seq))
             for distance in range(1, n_ctx):
                 grad_copy(peer(distance), me).start()
+            own_copy.start()
 
         return 0
 
@@ -358,10 +388,9 @@
     for distance in range(1, n_ctx):
         source = peer(n_ctx - distance)
         grad_copy(source, source).wait_recv()
-    for block in range(n_blocks):
-        for half in range(halves):
-            grad_res[half * SUB:(half + 1) * SUB, block * LANES:(block + 1) * LANES] = grad_all[block * halves + half]
-
+    own_copy.wait()
+    for group in range(n_groups):
+        store(group).wait()
     for distance in range(1, n_ctx):
         target = peer(distance)
         state_copy(target, me).wait_send()
@@ -372,26 +401,44 @@
         part_copy(seq_peer(distance), my_seq).wait_send()
 
 
-def writer(out_p, grad_query_p, grad_key_p, grad_value_p, grad_res, out, grad_query, grad_key, grad_value, grad_res_hbm, *scratch):
-    stage, sems, grad_sem = scratch[:4], scratch[4], scratch[5]
-    length, channels = out_p.shape
-    n_parts = sems.shape[1]
+def writer(
+    result, grad_all, out, grad_query, grad_key, grad_value, grad_res,
+    stage, turned, grad_tiles, grad_rows, load_sem, store_sem, grad_sem,
+):
+    length, channels = out.shape
+    n_parts = load_sem.shape[1]
     part = channels // n_parts
-    whole = pltpu.make_async_copy(grad_res, grad_res_hbm, grad_sem)
-    whole.start()
+    n_tiles = grad_all.shape[0]
+    halves = grad_res.shape[0] // SUB
+    targets = (out, grad_query, grad_key, grad_value)
+
+    def place_of(index, place):
+        return slice(index * length, (index + 1) * length), slice(place * part, (place + 1) * part)
+
+    loads, stores = {}, []
+    for place in range(n_parts):
+        for index in range(4):
+            where = place_of(index, place)
+            loads[index, place] = pltpu.make_async_copy(result.at[where], stage.at[where], load_sem.at[index, place])
+            loads[index, place].start()
+    grad_load = pltpu.make_async_copy(grad_all, grad_tiles, grad_sem.at[0])
+    grad_load.start()
     to_tokens = step_order(length, length // SUB, True)
-    copies = []
     for place in range(n_parts):
-        cols = slice(place * part, (place + 1) * part)
-        for index, (source, target) in enumerate(
-            zip((out_p, grad_query_p, grad_key_p, grad_value_p), (out, grad_query, grad_key, grad_value))
-        ):
-            stage[index][:, cols] = jnp.dot(to_tokens, source[:, cols], preferred_element_type=F32).astype(jnp.bfloat16)
-            copies.append(pltpu.make_async_copy(stage[index].at[:, cols], target.at[:, cols], sems.at[index, place]))
-            copies[-1].start()
-    for copy in copies:
+        for index in range(4):
+            where = place_of(index, place)
+            loads[index, place].wait()
+            turned[where] = jnp.dot(to_tokens, stage[where], preferred_element_type=F32).astype(jnp.bfloat16)
+            stores.append(pltpu.make_async_copy(turned.at[where], targets[index].at[:, where[1]], store_sem.at[index, place]))
+            stores[-1].start()
+    grad_load.wait()
+    for tile in range(n_tiles):
+        block, half = divmod(tile, halves)
+        grad_rows[half * SUB:(half + 1) * SUB, block * LANES:(block + 1) * LANES] = grad_tiles[tile]
+    stores.append(pltpu.make_async_copy(grad_rows, grad_res, grad_sem.at[1]))
+    stores[-1].start()
+    for copy in stores:
         copy.wait()
-    whole.wait()
 
 
 def on_device(n_ctx, n_seq, query_input, key_input, value_input, cotangent, residues, decay_rates):
@@ -409,17 +456,17 @@
         return pltpu.VMEM(leading + (SUB, LANES), F32)
 
     signal = jax.ShapeDtypeStruct((length, channels), jnp.bfloat16)
-    vmem = pl.BlockSpec(memory_space=pltpu.VMEM)
     hbm = pl.BlockSpec(memory_space=pltpu.HBM)
     n_parts = 4
     wide_rows = [pltpu.VMEM((length, channels), jnp.bfloat16) for _ in range(4)]
     results = pl.pallas_call(
         functools.partial(kernel, n_ctx, n_seq, n_parts),
-        out_shape=[signal] * 4 + [jax.ShapeDtypeStruct((modes, channels), F32)],
+        out_shape=[jax.ShapeDtypeStruct((4 * length, channels), jnp.bfloat16), jax.ShapeDtypeStruct((n_tiles, SUB, LANES), F32)],
         in_specs=[hbm] * 6,
-        out_specs=[vmem] * 5,
+        out_specs=[hbm] * 2,
         scratch_shapes=wide_rows
         + [pltpu.VMEM((modes, channels), F32) for _ in range(2)]
+        + [pltpu.VMEM((4 * length, channels), jnp.bfloat16)]
         + [rows() for _ in range(8)]
         + [tiles(n_tiles, SUB), tiles(n_tiles, SUB)]
         + [tiles(max(1, per_owner // halves), halves, SUB) for _ in range(2)]
@@ -429,14 +476,15 @@
             tiles(n_tiles, 2), tiles(n_ctx, per_owner, 2),
             tiles(n_ctx, per_owner, 2), tiles(n_tiles, 2),
             tiles(n_tiles), tiles(n_ctx, per_owner),
-            tiles(n_seq, per_owner), tiles(n_tiles),
+            tiles(n_seq, per_owner), tiles(per_owner),
         ]
         + [pltpu.SemaphoreType.DMA((n_ctx,)) for _ in range(6)]
         + [pltpu.SemaphoreType.DMA((n_seq,)) for _ in range(2)]
         + [pltpu.SemaphoreType.DMA((n_ctx,)) for _ in range(2)]
-        + [pltpu.SemaphoreType.DMA((4, n_parts)), pltpu.SemaphoreType.DMA((2,))],
+        + [pltpu.SemaphoreType.DMA((4, n_parts)), pltpu.SemaphoreType.DMA((2,))]
+        + [pltpu.SemaphoreType.DMA((n_ctx,)), pltpu.SemaphoreType.DMA],
         compiler_params=pltpu.CompilerParams(
-            collective_id=0, has_side_effects=True, vmem_limit_bytes=829 * 64 * 1024
+            collective_id=0, has_side_effects=True, vmem_limit_bytes=60 * 1024 * 1024
         ),
         cost_estimate=pl.CostEstimate(flops=100_000_000, bytes_accessed=4_500_000, transcendentals=1_000_000),
         name="modal_states",
@@ -444,10 +492,13 @@
     results = pl.pallas_call(
         writer,
         out_shape=[signal] * 4 + [jax.ShapeDtypeStruct((modes, channels), F32)],
-        in_specs=[vmem] * 5,
+        in_specs=[hbm] * 2,
         out_specs=[hbm] * 5,
-        scratch_shapes=wide_rows + [pltpu.SemaphoreType.DMA((4, n_parts)), pltpu.SemaphoreType.DMA],
-        compiler_params=pltpu.CompilerParams(vmem_limit_bytes=16 * 1024 * 1024),
+        scratch_shapes=[pltpu.VMEM((4 * length, channels), jnp.bfloat16) for _ in range(2)]
+        + [tiles(n_tiles), pltpu.VMEM((modes, channels), F32)]
+        + [pltpu.SemaphoreType.DMA((4, n_parts)) for _ in range(2)]
+        + [pltpu.SemaphoreType.DMA((2,))],
+        compiler_params=pltpu.CompilerParams(vmem_limit_bytes=60 * 1024 * 1024),
         cost_estimate=pl.CostEstimate(flops=300_000_000, bytes_accessed=4_500_000, transcendentals=0),
         name="token_order",
     )(*results)

time: 38.5 us -> 38.5 us (level)
  Pallas kernels: 34.8 us -> 37.7 us
  local copies, waits for them, and re-layouts: 2.84 us -> 0 us
    pallas_call x1, Pallas kernels: 1.67 us -> 4.73 us  [on_device(): pl.pallas_call(writer, out_shape=[signal] * 4 + [jax.ShapeDtypeStruct((mo...]
    unnamed x6 -> x0, local copies, waits for them, and re-layouts: 2.84 us -> none
where the time goes in v3:
time: 38.5 us; the launch traced here: 38.3 us
  Pallas kernels  37.7 us (98%)
  between operations  0.64 us (2%)
    pallas_call x1, Pallas kernels, on_device(): pl.pallas_call(functools.partial(kernel, n_ctx, n_seq, n_parts), out_shap...  33 us
    pallas_call x1, Pallas kernels, on_device(): pl.pallas_call(writer, out_shape=[signal] * 4 + [jax.ShapeDtypeStruct((mo...  4.73 us

profile of v3, /device:TPU:0, one launch (start us, length us, event | category | flops | bytes accessed | tf_op | source)
XLA Modules:
  0.0 38.3 jit_solution(12426220444604545738)
XLA Ops:
  0.6 33.0 %modal_states.1 = (bf16[512,2048]{1,0:T(8,128)(2,1)}, f32[32,8,128]{2,1,0:T(8,128)}) custom-call(bf16[128,2048]{1,0:T(8,128)(2,1)} %bitcast.11, bf16[128,2048]{1,0:T(8,128)(2,1)} %bitcast.12, bf16[128,2048]{1,0:T(8,128)(2,1)} %bitcast.13, bf16[128,2048]{1,0:T(8,128)(2,1)} %bitcast.14, f32[16,2048]{1,0:T(8,128)} %bitcast.15, f32[16,2048]{1,0:T(8,128)} %bitcast.16), custom_call_target="tpu_custom_call" | custom-call | flops 100000000 | bytes 4500000 | tf_op jit(solution)/shard_map/modal_states/pallas_call | solution.py:462
  33.6 4.7 %token_order.1 = (bf16[128,2048]{1,0:T(8,128)(2,1)}, bf16[128,2048]{1,0:T(8,128)(2,1)}, bf16[128,2048]{1,0:T(8,128)(2,1)}, bf16[128,2048]{1,0:T(8,128)(2,1)}, f32[16,2048]{1,0:T(8,128)}) custom-call(bf16[512,2048]{1,0:T(8,128)(2,1)} %get-tuple-element.12.result, f32[32,8,128]{2,1,0:T(8,128)} %get-tuple-element.13.grad_all), custom_call_target="tpu_custom_call" | custom-call | flops 300000000 | bytes 4500000 | tf_op jit(solution)/shard_map/token_order/pallas_call | solution.py:492

commit v4 on v3

v4 whole, which is shorter than its diff:
```python
import functools

import jax
import jax.numpy as jnp
from jax import lax
from jax.experimental import pallas as pl
from jax.experimental.pallas import tpu as pltpu
from jax.sharding import PartitionSpec as P

SUB = 8
LANES = 128
LOCAL = 4
MESH = pl.DeviceIdType.MESH
F32 = jnp.float32


def one_minus_exp(u):
    total = jnp.ones_like(u)
    for order in range(8, 1, -1):
        total = 1.0 - (u / order) * total
    return u * total


def columns_of(block):
    return pl.ds(pl.multiple_of(block * LANES, LANES), LANES)


def step_order(length, steps, inverse):
    row = lax.broadcasted_iota(jnp.int32, (length, length), 0)
    col = lax.broadcasted_iota(jnp.int32, (length, length), 1)
    if inverse:
        row, col = col, row
    return jnp.where(col == steps * (row % SUB) + row // SUB, 1.0, 0.0).astype(jnp.bfloat16)


def kernel(
    n_ctx, n_seq, n_parts, query_hbm, key_hbm, value_hbm, cot_hbm, param_ref,
    out, grad_query, grad_key, grad_value, grad_all,
    query, key, value, cot,
    query_p, key_p, value_p, cot_p, mix_p, adj_p, conv_p, back_p, before, after, up_turn, down_turn,
    lam_row, lam16_row, weight_row, rate_tile, scale_tile,
    state_out, state_in, carry_out, carry_in, hop_up, hop_down, hop_in,
    cross_out, cross_in, lag_out, lag_in, part_in, grad_own,
    state_send, state_recv, carry_send, carry_recv, hop_send, hop_recv, cross_send, cross_recv,
    lag_send, lag_recv, grad_send, grad_recv, part_send, part_recv, load_sem, own_sem,
):
    me = lax.axis_index("ctx")
    my_seq = lax.axis_index("seq")
    length, channels = query.shape
    modes = param_ref.shape[0] // 2
    steps = length // SUB
    n_blocks = channels // LANES
    halves = modes // SUB
    n_tiles = n_blocks * halves
    n_groups = n_ctx // LOCAL
    my_group, my_local = me // LOCAL, lax.rem(me, LOCAL)
    per_owner = n_tiles // LOCAL
    per_sum = per_owner // n_groups
    owner_blocks = per_owner // halves
    piece_blocks = max(1, owner_blocks // 2)
    owner_pieces = owner_blocks // piece_blocks
    piece_tiles = piece_blocks * halves
    n_pieces = n_blocks // piece_blocks
    part = channels // n_parts

    def load(index, place):
        cols = pl.ds(pl.multiple_of(place * part, LANES), part)
        source = (key_hbm, value_hbm, query_hbm, cot_hbm)[index]
        target = (key, value, query, cot)[index]
        return pltpu.make_async_copy(source.at[:, cols], target.at[:, cols], load_sem.at[index, place])

    for place in range(n_parts):
        for index in range(4):
            load(index, place).start()

    def peer(distance):
        return lax.rem(me + distance, n_ctx)

    def seq_peer(distance):
        return lax.rem(my_seq + distance, n_seq)

    def remote(src, dst, send, recv, target):
        return pltpu.make_async_remote_copy(
            src_ref=src, dst_ref=dst, send_sem=send, recv_sem=recv,
            device_id=target, device_id_type=MESH,
        )

    def piece_of(ref, piece):
        return ref.at[pl.ds(piece * piece_tiles, piece_tiles)]

    def sum_start(owner):
        return lax.rem(owner, LOCAL) * per_owner + owner // LOCAL * per_sum

    def summed(ref, owner):
        return ref.at[pl.ds(sum_start(owner), per_sum)]

    def state_copy(owner, place, slot):
        return remote(
            piece_of(state_out, owner * owner_pieces + place), piece_of(state_in.at[slot], place),
            state_send.at[owner, place], state_recv.at[slot, place], {"ctx": my_group * LOCAL + owner},
        )

    def carry_copy(target, place, slot):
        return remote(
            piece_of(carry_out.at[target], place), piece_of(carry_in, slot * owner_pieces + place),
            carry_send.at[target, place], carry_recv.at[slot, place], {"ctx": my_group * LOCAL + target},
        )

    def hop_copy(source, target, slot):
        return remote(source, hop_in.at[slot], hop_send.at[target], hop_recv.at[slot], {"ctx": target * LOCAL + my_local})

    def cross_copy(target, slot):
        return remote(
            cross_out.at[pl.ds(target * per_sum, per_sum)], cross_in.at[slot],
            cross_send.at[target], cross_recv.at[slot], {"ctx": target * LOCAL + my_local},
        )

    def lag_copy(owner, slot):
        return remote(summed(lag_out, owner), lag_in.at[slot], lag_send.at[owner], lag_recv.at[slot], {"ctx": owner})

    def part_copy(target, slot):
        return remote(part_in.at[my_seq], part_in.at[slot], part_send.at[target], part_recv.at[slot], {"seq": target})

    def grad_copy(target, slot):
        return remote(grad_own, summed(grad_all, slot), grad_send.at[target], grad_recv.at[slot], {"ctx": target})

    barrier = pltpu.get_barrier_semaphore()
    for distance in range(1, n_ctx):
        pl.semaphore_signal(barrier, inc=1, device_id={"ctx": peer(distance)}, device_id_type=MESH)
    for distance in range(1, n_seq):
        pl.semaphore_signal(barrier, inc=1, device_id={"seq": seq_peer(distance)}, device_id_type=MESH)

    for block in range(n_blocks):
        cols = slice(block * LANES, (block + 1) * LANES)
        rate = param_ref[:modes, cols]
        scale = jnp.sqrt(one_minus_exp(2.0 * rate))
        lam_row[block] = jnp.exp(-rate)
        lam16_row[block] = jnp.exp(-float(steps) * rate)
        weight_row[block] = param_ref[modes:, cols] * scale
        for half in range(halves):
            rows = slice(half * SUB, (half + 1) * SUB)
            rate_tile[block * halves + half] = rate[rows]
            scale_tile[block * halves + half] = scale[rows]

    to_steps = step_order(length, steps, False)

    def turn(place, _):
        cols = pl.ds(pl.multiple_of(place * part, LANES), part)
        for index in range(4):
            load(index, place).wait()
        key_here, value_here, query_here, cot_here = [
            jnp.dot(to_steps, ref[:, cols], preferred_element_type=F32) for ref in (key, value, query, cot)
        ]
        mixed = key_here * value_here
        adjoint = cot_here * query_here
        for inner in range(part // LANES):
            block = place * (part // LANES) + inner
            lanes = slice(inner * LANES, (inner + 1) * LANES)
            query_p[block] = query_here[:, lanes]
            key_p[block] = key_here[:, lanes]
            value_p[block] = value_here[:, lanes]
            cot_p[block] = cot_here[:, lanes]
            mix_p[block] = mixed[:, lanes]
            adj_p[block] = adjoint[:, lanes]
        return 0

    lax.fori_loop(0, n_parts, turn, 0)

    def wide(ref, block, mode):
        return jnp.broadcast_to(ref[block, pl.ds(mode, 1), :], (SUB, LANES))

    def half_rows(ref, block, half):
        return ref[block, half * SUB:(half + 1) * SUB, :]

    def rows_at(ref, block, step):
        return ref[block, step * SUB:(step + 1) * SUB, :]

    def tree(terms):
        while len(terms) > 1:
            terms = [sum(terms[place:place + 2][1:], terms[place]) for place in range(0, len(terms), 2)]
        return terms[0]

    def cut(array):
        return [array[step * SUB:(step + 1) * SUB] for step in range(steps)]

    def states_of(block, inner):
        for half in range(halves):
            lams = [wide(lam_row, block, half * SUB + mode) for mode in range(SUB)]
            lasts = [rows_at(mix_p, block, 0)] * SUB
            firsts = [rows_at(adj_p, block, steps - 1)] * SUB
            for step in range(1, steps):
                mix, adj = rows_at(mix_p, block, step), rows_at(adj_p, block, steps - 1 - step)
                lasts = [have * lam + mix for have, lam in zip(lasts, lams)]
                firsts = [have * lam + adj for have, lam in zip(firsts, lams)]
            for mode in range(SUB):
                up_turn[inner, half, mode] = lasts[mode]
                down_turn[inner, half, mode] = firsts[mode]
        for half in range(halves):
            tile = block * halves + half
            lam16 = half_rows(lam16_row, block, half)
            lasts = [up_turn[inner, half, :, chunk, :] for chunk in range(SUB)]
            firsts = [down_turn[inner, half, :, chunk, :] for chunk in range(SUB)]
            state = lasts[0]
            lag = jnp.zeros_like(state)
            for chunk in range(1, SUB):
                before[tile, chunk] = state
                lag = lag + firsts[chunk] * state
                state = state * lam16 + lasts[chunk]
            state_out[tile, 0] = state
            lag_out[tile] = lag
            state = firsts[-1]
            for chunk in range(SUB - 2, -1, -1):
                after[tile, chunk] = state
                state = state * lam16 + firsts[chunk]
            state_out[tile, 1] = state

    def first_pass(index, _):
        piece = lax.rem(owner_pieces * (my_local + 1) + index, n_pieces)
        for inner in range(piece_blocks):
            states_of(piece * piece_blocks + inner, inner)

        @pl.when(index == 0)
        def _():
            pl.semaphore_wait(barrier, n_ctx - 1 + n_seq - 1)

        owner, place = piece // owner_pieces, lax.rem(piece, owner_pieces)

        @pl.when(owner != my_local)
        def _():
            state_copy(owner, place, my_local).start()

        @pl.when(owner == my_local)
        def _():
            state_in[my_local, pl.ds(place * piece_tiles, piece_tiles)] = state_out[pl.ds(piece * piece_tiles, piece_tiles)]

        return 0

    lax.fori_loop(0, n_pieces, first_pass, 0)

    def chunk_terms(block):
        mix = cut(mix_p[block])
        adj = cut(adj_p[block])
        lam = [lam_row[block, pl.ds(half * SUB, SUB), :] for half in range(halves)]
        power = [weight_row[block, pl.ds(half * SUB, SUB), :] for half in range(halves)]
        taps = []
        for step in range(steps):
            taps.append(jnp.broadcast_to(jnp.sum(sum(power), axis=0, keepdims=True), (SUB, LANES)))
            power = [left * right for left, right in zip(power, lam)]
        totals = [taps[0] * rows for rows in mix]
        for lag in range(1, steps):
            for step in range(lag, steps):
                totals[step] = totals[step] + taps[lag] * mix[step - lag]
        for step in range(steps):
            conv_p[block, step * SUB:(step + 1) * SUB, :] = totals[step]
        totals = [taps[0] * rows for rows in adj]
        for lag in range(1, steps):
            for step in range(steps - lag):
                totals[step] = totals[step] + taps[lag] * adj[step + lag]
        for step in range(steps):
            back_p[block, step * SUB:(step + 1) * SUB, :] = totals[step]
        totals = [rows * mix[0] for rows in adj]
        for step in range(1, steps):
            for lag in range(steps - step):
                totals[lag] = totals[lag] + adj[step + lag] * mix[step]
        levels = [jnp.broadcast_to(jnp.sum(total, axis=0, keepdims=True), (SUB, LANES)) for total in totals]
        sums = [levels[-1]] * halves
        for level in levels[-2::-1]:
            sums = [have * left + level for have, left in zip(sums, lam)]
        for half in range(halves):
            tile = block * halves + half
            lag_out[tile] = sums[half] + lam[half] * lag_out[tile]

    def second_pass(index, _):
        piece = lax.rem(owner_pieces * (my_local + 1) + index, n_pieces)
        for inner in range(piece_blocks):
            chunk_terms(piece * piece_blocks + inner)
        for inner in range(piece_tiles // per_sum):
            start = piece * piece_tiles + inner * per_sum
            owner = lax.rem(start, per_owner) // per_sum * LOCAL + start // per_owner

            @pl.when(owner != me)
            def _():
                lag_copy(owner, me).start()

            @pl.when(owner == me)
            def _():
                lag_in[me] = lag_out[pl.ds(sum_start(me), per_sum)]

        return 0

    lax.fori_loop(0, n_pieces // 4, second_pass, 0)

    def local_peer(distance):
        return lax.rem(my_local + distance, LOCAL)

    def group_peer(distance):
        return lax.rem(my_group + distance, n_groups)

    for distance in range(1, LOCAL):
        source = local_peer(LOCAL - distance)
        for place in range(owner_pieces):
            state_copy(source, place, source).wait_recv()
    my_first = my_local * per_owner
    for place in range(per_owner):
        hop = jnp.exp(-float(length) * rate_tile[my_first + place])
        carried = state_in[0, place, 0]
        for source in range(1, LOCAL):
            carry_out[source, place, 0] = carried
            carried = carried * hop + state_in[source, place, 0]
        hop_up[place] = carried
        carried = state_in[LOCAL - 1, place, 1]
        for source in range(LOCAL - 2, -1, -1):
            carry_out[source, place, 1] = carried
            carried = carried * hop + state_in[source, place, 1]
        hop_down[place] = carried
    for distance in range(1, n_groups):
        target = group_peer(distance)

        @pl.when(target > my_group)
        def _():
            hop_copy(hop_up, target, my_group).start()

        @pl.when(target < my_group)
        def _():
            hop_copy(hop_down, target, my_group).start()

    hop_in[my_group] = jnp.zeros((per_owner, SUB, LANES), F32)

    lax.fori_loop(n_pieces // 4, 3 * n_pieces // 4, second_pass, 0)

    for distance in range(1, n_groups):
        source = group_peer(n_groups - distance)
        hop_copy(hop_up, source, source).wait_recv()
    for place in range(per_owner):
        rate = rate_tile[my_first + place]
        hop = jnp.exp(-float(length) * rate)
        far = jnp.exp(-float(length * LOCAL) * rate)
        carried = jnp.zeros((SUB, LANES), F32)
        for group in range(n_groups):
            carried = jnp.where(group < my_group, carried * far + hop_in[group, place], carried)
        cross = jnp.zeros((SUB, LANES), F32)
        for source in range(LOCAL):
            total = carry_out[source, place, 0] + carried if source else carried
            carry_out[source, place, 0] = total
            cross = cross + total * state_in[source, place, 1]
            carried = carried * hop
        cross_out[place] = jnp.exp(-rate) * cross
        carried = jnp.zeros((SUB, LANES), F32)
        for group in range(n_groups - 1, -1, -1):
            carried = jnp.where(group > my_group, carried * far + hop_in[group, place], carried)
        for source in range(LOCAL - 1, -1, -1):
            carry_out[source, place, 1] = carry_out[source, place, 1] + carried if source < LOCAL - 1 else carried
            carried = carried * hop
    for place in range(owner_pieces):
        for distance in range(1, LOCAL):
            carry_copy(local_peer(distance), place, my_local).start()
    for distance in range(1, n_groups):
        cross_copy(group_peer(distance), my_group).start()
    carry_in[pl.ds(my_first, per_owner)] = carry_out[my_local]
    cross_in[my_group] = cross_out[pl.ds(my_group * per_sum, per_sum)]

    lax.fori_loop(3 * n_pieces // 4, n_pieces, second_pass, 0)

    def finish(block, inner):
        cols = columns_of(block)
        for half in range(halves):
            tile = block * halves + half
            lam16 = half_rows(lam16_row, block, half)
            lead = half_rows(lam_row, block, half) * half_rows(weight_row, block, half)
            state = carry_in[tile, 0]
            for chunk in range(SUB):
                up_turn[inner, half, chunk] = lead * (state + before[tile, chunk] if chunk else state)
                state = state * lam16
            state = carry_in[tile, 1]
            for chunk in range(SUB - 1, -1, -1):
                down_turn[inner, half, chunk] = lead * (state + after[tile, chunk] if chunk < SUB - 1 else state)
                state = state * lam16
        lams = [wide(lam_row, block, mode) for mode in range(modes)]

        def put(place, step, factor, pair):
            rows = pl.ds(step * SUB, 2 * SUB)
            target = (out, grad_query, grad_key, grad_value)[place]
            target[rows, cols] = (factor[block, rows, :] * pair).astype(jnp.bfloat16)

        terms = [up_turn[inner, mode // SUB, :, mode % SUB, :] for mode in range(modes)]
        sums = []
        for step in range(steps):
            sums.append(rows_at(conv_p, block, step) + tree(terms))
            terms = [term * lam for term, lam in zip(terms, lams)]
            if step % 2:
                pair = jnp.concatenate(sums, axis=0)
                put(0, step - 1, query_p, pair)
                put(1, step - 1, cot_p, pair)
                sums = []
        terms = [down_turn[inner, mode // SUB, :, mode % SUB, :] for mode in range(modes)]
        for step in range(steps - 1, -1, -1):
            sums.insert(0, rows_at(back_p, block, step) + tree(terms))
            terms = [term * lam for term, lam in zip(terms, lams)]
            if step % 2 == 0:
                pair = jnp.concatenate(sums, axis=0)
                put(2, step, value_p, pair)
                put(3, step, key_p, pair)
                sums = []

    own_copy = pltpu.make_async_copy(grad_own, summed(grad_all, me), own_sem)

    def last_pass(index, _):
        owner = lax.rem(my_local + LOCAL - index // owner_pieces, LOCAL)
        place = lax.rem(index, owner_pieces)

        @pl.when(owner != my_local)
        def _():
            carry_copy(owner, place, owner).wait_recv()

        for inner in range(piece_blocks):
            finish((owner * owner_pieces + place) * piece_blocks + inner, inner)

        @pl.when(index == n_pieces // 4)
        def _():
            for distance in range(1, n_ctx):
                source = peer(n_ctx - distance)
                lag_copy(source, source).wait_recv()
            for distance in range(1, n_groups):
                source = group_peer(n_groups - distance)
                cross_copy(source, source).wait_recv()
            for place in range(per_sum):
                total = lag_in[0, place]
                for source in range(1, n_ctx):
                    total = total + lag_in[source, place]
                for source in range(n_groups):
                    total = total + cross_in[source, place]
                part_in[my_seq, place] = total * scale_tile[sum_start(me) + place]
            for distance in range(1, n_seq):
                part_copy(seq_peer(distance), my_seq).start()

        @pl.when(index == 5 * n_pieces // 8)
        def _():
            for distance in range(1, n_seq):
                source = seq_peer(n_seq - distance)
                part_copy(source, source).wait_recv()
            for place in range(per_sum):
                total = part_in[0, place]
                for source in range(1, n_seq):
                    total = total + part_in[source, place]
                grad_own[place] = total * (1.0 / (length * n_ctx * n_seq))
            for distance in range(1, n_ctx):
                grad_copy(peer(distance), me).start()
            own_copy.start()

        return 0

    lax.fori_loop(0, n_pieces, last_pass, 0)

    for distance in range(1, n_ctx):
        source = peer(n_ctx - distance)
        grad_copy(source, source).wait_recv()
    own_copy.wait()
    for distance in range(1, n_ctx):
        target = peer(distance)
        lag_copy(target, me).wait_send()
        grad_copy(target, me).wait_send()
    for distance in range(1, LOCAL):
        target = local_peer(distance)
        for place in range(owner_pieces):
            state_copy(target, place, my_local).wait_send()
            carry_copy(target, place, my_local).wait_send()
    for distance in range(1, n_groups):
        target = group_peer(distance)
        hop_copy(hop_up, target, my_group).wait_send()
        cross_copy(target, my_group).wait_send()
    for distance in range(1, n_seq):
        part_copy(seq_peer(distance), my_seq).wait_send()


def writer(
    out_p, grad_query_p, grad_key_p, grad_value_p, grad_tiles, out, grad_query, grad_key, grad_value, grad_res,
    turned, grad_rows, store_sem, grad_sem,
):
    length, channels = out.shape
    n_parts = store_sem.shape[1]
    part = channels // n_parts
    halves = grad_res.shape[0] // SUB
    sources = (out_p, grad_query_p, grad_key_p, grad_value_p)
    targets = (out, grad_query, grad_key, grad_value)
    for tile in range(grad_tiles.shape[0]):
        block, half = divmod(tile, halves)
        grad_rows[half * SUB:(half + 1) * SUB, block * LANES:(block + 1) * LANES] = grad_tiles[tile]
    stores = [pltpu.make_async_copy(grad_rows, grad_res, grad_sem)]
    stores[-1].start()
    to_tokens = step_order(length, length // SUB, True)
    for place in range(n_parts):
        cols = slice(place * part, (place + 1) * part)
        for index in range(4):
            where = (slice(index * length, (index + 1) * length), cols)
            turned[where] = jnp.dot(to_tokens, sources[index][:, cols], preferred_element_type=F32).astype(jnp.bfloat16)
            stores.append(pltpu.make_async_copy(turned.at[where], targets[index].at[:, cols], store_sem.at[index, place]))
            stores[-1].start()
    for copy in stores:
        copy.wait()


def on_device(n_ctx, n_seq, query_input, key_input, value_input, cotangent, residues, decay_rates):
    _, length, channels = query_input.shape
    modes = residues.shape[1]
    n_blocks = channels // LANES
    halves = modes // SUB
    n_tiles = n_blocks * halves
    n_groups = n_ctx // LOCAL
    per_owner = n_tiles // LOCAL
    per_sum = per_owner // n_groups
    piece_blocks = max(1, per_owner // halves // 2)
    owner_pieces = per_owner // halves // piece_blocks

    def rows():
        return pltpu.VMEM((n_blocks, length, LANES), F32)

    def tiles(*leading):
        return pltpu.VMEM(leading + (SUB, LANES), F32)

    signal = jax.ShapeDtypeStruct((length, channels), jnp.bfloat16)
    hbm = pl.BlockSpec(memory_space=pltpu.HBM)
    vmem = pl.BlockSpec(memory_space=pltpu.VMEM)
    n_parts = 4
    wide_rows = [pltpu.VMEM((length, channels), jnp.bfloat16) for _ in range(4)]
    results = pl.pallas_call(
        functools.partial(kernel, n_ctx, n_seq, n_parts),
        out_shape=[signal] * 4 + [jax.ShapeDtypeStruct((n_tiles, SUB, LANES), F32)],
        in_specs=[hbm] * 4 + [vmem],
        out_specs=[vmem] * 5,
        scratch_shapes=wide_rows
        + [rows() for _ in range(8)]
        + [tiles(n_tiles, SUB), tiles(n_tiles, SUB)]
        + [tiles(piece_blocks, halves, SUB) for _ in range(2)]
        + [pltpu.VMEM((n_blocks, modes, LANES), F32) for _ in range(3)]
        + [tiles(n_tiles), tiles(n_tiles)]
        + [
            tiles(n_tiles, 2), tiles(LOCAL, per_owner, 2), tiles(LOCAL, per_owner, 2), tiles(n_tiles, 2),
            tiles(per_owner), tiles(per_owner), tiles(n_groups, per_owner),
            tiles(per_owner), tiles(n_groups, per_sum), tiles(n_tiles), tiles(n_ctx, per_sum),
            tiles(n_seq, per_sum), tiles(per_sum),
        ]
        + [pltpu.SemaphoreType.DMA((LOCAL, owner_pieces)) for _ in range(4)]
        + [pltpu.SemaphoreType.DMA((n_groups,)) for _ in range(4)]
        + [pltpu.SemaphoreType.DMA((n_ctx,)) for _ in range(4)]
        + [pltpu.SemaphoreType.DMA((n_seq,)) for _ in range(2)]
        + [pltpu.SemaphoreType.DMA((4, n_parts)), pltpu.SemaphoreType.DMA],
        compiler_params=pltpu.CompilerParams(
            collective_id=0, has_side_effects=True, vmem_limit_bytes=820 * 64 * 1024
        ),
        cost_estimate=pl.CostEstimate(flops=100_000_000, bytes_accessed=4_500_000, transcendentals=1_000_000),
        name="modal_states",
    )(query_input[0], key_input[0], value_input[0], cotangent[0], jnp.concatenate([decay_rates.T, residues.T], axis=0))
    results = pl.pallas_call(
        writer,
        out_shape=[signal] * 4 + [jax.ShapeDtypeStruct((modes, channels), F32)],
        in_specs=[vmem] * 5,
        out_specs=[hbm] * 5,
        scratch_shapes=[
            pltpu.VMEM((4 * length, channels), jnp.bfloat16), pltpu.VMEM((modes, channels), F32),
            pltpu.SemaphoreType.DMA((4, n_parts)), pltpu.SemaphoreType.DMA,
        ],
        compiler_params=pltpu.CompilerParams(vmem_limit_bytes=16 * 1024 * 1024),
        cost_estimate=pl.CostEstimate(flops=300_000_000, bytes_accessed=4_500_000, transcendentals=0),
        name="token_order",
    )(*results)
    return tuple(array[None] for array in results[:4]) + (results[4].T,)


def solution(mesh):
    wide = P("seq", "ctx", None)
    return jax.shard_map(
        functools.partial(on_device, mesh.shape["ctx"], mesh.shape["seq"]),
        mesh=mesh,
        in_specs=(wide, wide, wide, wide, P(), P()),
        out_specs=(wide, wide, wide, wide, P()),
        check_vma=False,
    )
```

time: 38.5 us -> 32.5 us (0.84)
  Pallas kernels: 37.7 us -> 30.7 us
  other arithmetic: 0 us -> 0.99 us
    pallas_call x1, Pallas kernels: 33 us -> 29 us  [on_device(): pl.pallas_call(functools.partial(kernel, n_ctx, n_seq, n_parts), out_shap...]
    pallas_call x1, Pallas kernels: 4.73 us -> 1.68 us  [on_device(): pl.pallas_call(writer, out_shape=[signal] * 4 + [jax.ShapeDtypeStruct((mo...]
    concatenate x0 -> x1, other arithmetic: none -> 0.99 us  [on_device(): jnp.concatenate([decay_rates.T, residues.T], axis=0)]
where the time goes in v4:
time: 32.5 us; the launch traced here: 32.3 us
  Pallas kernels  30.7 us (94%)
  other arithmetic  0.99 us (3%)
  between operations  0.64 us (2%)
    pallas_call x1, Pallas kernels, on_device(): pl.pallas_call(functools.partial(kernel, n_ctx, n_seq, n_parts), out_shap...  29 us
    pallas_call x1, Pallas kernels, on_device(): pl.pallas_call(writer, out_shape=[signal] * 4 + [jax.ShapeDtypeStruct((mo...  1.68 us
    concatenate x1, other arithmetic, on_device(): jnp.concatenate([decay_rates.T, residues.T], axis=0)  0.99 us

profile of v4, /device:TPU:0, one launch (start us, length us, event | category | flops | bytes accessed | tf_op | source)
XLA Modules:
  0.0 32.3 jit_solution(17261322295467632379)
XLA Ops:
  0.6 1.0 %pad_maximum_fusion.param_ref = f32[32,2048]{1,0:T(8,128)S(1)} fusion(f32[16,2048]{1,0:T(8,128)} %bitcast.15, f32[16,2048]{1,0:T(8,128)} %bitcast.16), kind=kLoop, calls=%fused_computation | loop fusion | flops 65536 | bytes 524288 | tf_op jit(solution)/shard_map/concatenate | solution.py:552
  1.6 29.0 %modal_states.1 = (bf16[128,2048]{1,0:T(8,128)(2,1)S(1)}, bf16[128,2048]{1,0:T(8,128)(2,1)S(1)}, bf16[128,2048]{1,0:T(8,128)(2,1)S(1)}, bf16[128,2048]{1,0:T(8,128)(2,1)S(1)}, f32[32,8,128]{2,1,0:T(8,128)S(1)}) custom-call(bf16[128,2048]{1,0:T(8,128)(2,1)} %bitcast.11, bf16[128,2048]{1,0:T(8,128)(2,1)} %bitcast.12, bf16[128,2048]{1,0:T(8,128)(2,1)} %bitcast.13, ...), custom_call_target="tpu_custom_call" | custom-call | flops 100000000 | bytes 4500000 | tf_op jit(solution)/shard_map/modal_states/pallas_call | solution.py:525
  30.6 1.7 %token_order.1 = (bf16[128,2048]{1,0:T(8,128)(2,1)}, bf16[128,2048]{1,0:T(8,128)(2,1)}, bf16[128,2048]{1,0:T(8,128)(2,1)}, bf16[128,2048]{1,0:T(8,128)(2,1)}, f32[16,2048]{1,0:T(8,128)}) custom-call(bf16[128,2048]{1,0:T(8,128)(2,1)S(1)} %get-tuple-element.15.out_p, bf16[128,2048]{1,0:T(8,128)(2,1)S(1)} %get-tuple-element.16.grad_query_p, ...), custom_call_target="tpu_custom_call" | custom-call | flops 300000000 | bytes 4500000 | tf_op jit(solution)/shard_map/token_order/pallas_call | solution.py:553

commit v5 on v4

--- a/solution.py
+++ b/solution.py
@@ -40,9 +40,9 @@
     query_p, key_p, value_p, cot_p, mix_p, adj_p, conv_p, back_p, before, after, up_turn, down_turn,
     lam_row, lam16_row, weight_row, rate_tile, scale_tile,
     state_out, state_in, carry_out, carry_in, hop_up, hop_down, hop_in,
-    cross_out, cross_in, lag_out, lag_in, part_in, grad_own,
+    cross_out, cross_in, lag_out, lag_in, grad_own,
     state_send, state_recv, carry_send, carry_recv, hop_send, hop_recv, cross_send, cross_recv,
-    lag_send, lag_recv, grad_send, grad_recv, part_send, part_recv, load_sem, own_sem,
+    lag_send, lag_recv, grad_send, grad_recv, load_sem, own_sem,
 ):
     me = lax.axis_index("ctx")
     my_seq = lax.axis_index("seq")
@@ -109,17 +109,15 @@
     def hop_copy(source, target, slot):
         return remote(source, hop_in.at[slot], hop_send.at[target], hop_recv.at[slot], {"ctx": target * LOCAL + my_local})
 
-    def cross_copy(target, slot):
+    def cross_copy(target, target_seq, slot):
         return remote(
             cross_out.at[pl.ds(target * per_sum, per_sum)], cross_in.at[slot],
-            cross_send.at[target], cross_recv.at[slot], {"ctx": target * LOCAL + my_local},
+            cross_send.at[target * n_seq + target_seq], cross_recv.at[slot],
+            {"ctx": target * LOCAL + my_local, "seq": target_seq},
         )
 
     def lag_copy(owner, slot):
         return remote(summed(lag_out, owner), lag_in.at[slot], lag_send.at[owner], lag_recv.at[slot], {"ctx": owner})
-
-    def part_copy(target, slot):
-        return remote(part_in.at[my_seq], part_in.at[slot], part_send.at[target], part_recv.at[slot], {"seq": target})
 
     def grad_copy(target, slot):
         return remote(grad_own, summed(grad_all, slot), grad_send.at[target], grad_recv.at[slot], {"ctx": target})
@@ -128,7 +126,9 @@
     for distance in range(1, n_ctx):
         pl.semaphore_signal(barrier, inc=1, device_id={"ctx": peer(distance)}, device_id_type=MESH)
     for distance in range(1, n_seq):
-        pl.semaphore_signal(barrier, inc=1, device_id={"seq": seq_peer(distance)}, device_id_type=MESH)
+        for group in range(n_groups):
+            target = {"ctx": lax.rem(my_group + group, n_groups) * LOCAL + my_local, "seq": seq_peer(distance)}
+            pl.semaphore_signal(barrier, inc=1, device_id=target, device_id_type=MESH)
 
     for block in range(n_blocks):
         cols = slice(block * LANES, (block + 1) * LANES)
@@ -221,7 +221,7 @@
 
         @pl.when(index == 0)
         def _():
-            pl.semaphore_wait(barrier, n_ctx - 1 + n_seq - 1)
+            pl.semaphore_wait(barrier, n_ctx - 1 + (n_seq - 1) * n_groups)
 
         owner, place = piece // owner_pieces, lax.rem(piece, owner_pieces)
 
@@ -236,6 +236,22 @@
         return 0
 
     lax.fori_loop(0, n_pieces, first_pass, 0)
+
+    def lag_terms(block):
+        mix = cut(mix_p[block])
+        adj = cut(adj_p[block])
+        lam = [lam_row[block, pl.ds(half * SUB, SUB), :] for half in range(halves)]
+        totals = [rows * mix[0] for rows in adj]
+        for step in range(1, steps):
+            for lag in range(steps - step):
+                totals[lag] = totals[lag] + adj[step + lag] * mix[step]
+        levels = [jnp.broadcast_to(jnp.sum(total, axis=0, keepdims=True), (SUB, LANES)) for total in totals]
+        sums = [levels[-1]] * halves
+        for level in levels[-2::-1]:
+            sums = [have * left + level for have, left in zip(sums, lam)]
+        for half in range(halves):
+            tile = block * halves + half
+            lag_out[tile] = sums[half] + lam[half] * lag_out[tile]
 
     def chunk_terms(block):
         mix = cut(mix_p[block])
@@ -258,22 +274,10 @@
                 totals[step] = totals[step] + taps[lag] * adj[step + lag]
         for step in range(steps):
             back_p[block, step * SUB:(step + 1) * SUB, :] = totals[step]
-        totals = [rows * mix[0] for rows in adj]
-        for step in range(1, steps):
-            for lag in range(steps - step):
-                totals[lag] = totals[lag] + adj[step + lag] * mix[step]
-        levels = [jnp.broadcast_to(jnp.sum(total, axis=0, keepdims=True), (SUB, LANES)) for total in totals]
-        sums = [levels[-1]] * halves
-        for level in levels[-2::-1]:
-            sums = [have * left + level for have, left in zip(sums, lam)]
-        for half in range(halves):
-            tile = block * halves + half
-            lag_out[tile] = sums[half] + lam[half] * lag_out[tile]
-
-    def second_pass(index, _):
+    def lag_pass(index, _):
         piece = lax.rem(owner_pieces * (my_local + 1) + index, n_pieces)
         for inner in range(piece_blocks):
-            chunk_terms(piece * piece_blocks + inner)
+            lag_terms(piece * piece_blocks + inner)
         for inner in range(piece_tiles // per_sum):
             start = piece * piece_tiles + inner * per_sum
             owner = lax.rem(start, per_owner) // per_sum * LOCAL + start // per_owner
@@ -288,7 +292,12 @@
 
         return 0
 
-    lax.fori_loop(0, n_pieces // 4, second_pass, 0)
+    lax.fori_loop(0, n_pieces, lag_pass, 0)
+
+    def second_pass(piece, _):
+        for inner in range(piece_blocks):
+            chunk_terms(piece * piece_blocks + inner)
+        return 0
 
     def local_peer(distance):
         return lax.rem(my_local + distance, LOCAL)
@@ -326,7 +335,7 @@
 
     hop_in[my_group] = jnp.zeros((per_owner, SUB, LANES), F32)
 
-    lax.fori_loop(n_pieces // 4, 3 * n_pieces // 4, second_pass, 0)
+    lax.fori_loop(0, 5 * n_pieces // 8, second_pass, 0)
 
     for distance in range(1, n_groups):
         source = group_peer(n_groups - distance)
@@ -354,12 +363,23 @@
     for place in range(owner_pieces):
         for distance in range(1, LOCAL):
             carry_copy(local_peer(distance), place, my_local).start()
-    for distance in range(1, n_groups):
-        cross_copy(group_peer(distance), my_group).start()
     carry_in[pl.ds(my_first, per_owner)] = carry_out[my_local]
-    cross_in[my_group] = cross_out[pl.ds(my_group * per_sum, per_sum)]
-
-    lax.fori_loop(3 * n_pieces // 4, n_pieces, second_pass, 0)
+
+    for distance in range(1, n_ctx):
+        source = peer(n_ctx - distance)
+        lag_copy(source, source).wait_recv()
+    for place in range(per_sum):
+        total = cross_out[my_group * per_sum + place]
+        for source in range(n_ctx):
+            total = total + lag_in[source, place]
+        cross_out[my_group * per_sum + place] = total
+    counterparts = [(group, seq) for group in range(n_groups) for seq in range(n_seq)][1:]
+    my_slot = my_group * n_seq + my_seq
+    for group, seq in counterparts:
+        cross_copy(group_peer(group), seq_peer(seq), my_slot).start()
+    cross_in[my_slot] = cross_out[pl.ds(my_group * per_sum, per_sum)]
+
+    lax.fori_loop(5 * n_pieces // 8, n_pieces, second_pass, 0)
 
     def finish(block, inner):
         cols = columns_of(block)
@@ -415,34 +435,16 @@
         for inner in range(piece_blocks):
             finish((owner * owner_pieces + place) * piece_blocks + inner, inner)
 
-        @pl.when(index == n_pieces // 4)
-        def _():
-            for distance in range(1, n_ctx):
-                source = peer(n_ctx - distance)
-                lag_copy(source, source).wait_recv()
-            for distance in range(1, n_groups):
-                source = group_peer(n_groups - distance)
-                cross_copy(source, source).wait_recv()
+        @pl.when(index == n_pieces // 2)
+        def _():
+            for group, seq in counterparts:
+                source, source_seq = group_peer(n_groups - group), seq_peer(n_seq - seq)
+                cross_copy(source, source_seq, source * n_seq + source_seq).wait_recv()
             for place in range(per_sum):
-                total = lag_in[0, place]
-                for source in range(1, n_ctx):
-                    total = total + lag_in[source, place]
-                for source in range(n_groups):
+                total = cross_in[0, place]
+                for source in range(1, n_groups * n_seq):
                     total = total + cross_in[source, place]
-                part_in[my_seq, place] = total * scale_tile[sum_start(me) + place]
-            for distance in range(1, n_seq):
-                part_copy(seq_peer(distance), my_seq).start()
-
-        @pl.when(index == 5 * n_pieces // 8)
-        def _():
-            for distance in range(1, n_seq):
-                source = seq_peer(n_seq - distance)
-                part_copy(source, source).wait_recv()
-            for place in range(per_sum):
-                total = part_in[0, place]
-                for source in range(1, n_seq):
-                    total = total + part_in[source, place]
-                grad_own[place] = total * (1.0 / (length * n_ctx * n_seq))
+                grad_own[place] = total * scale_tile[sum_start(me) + place] * (1.0 / (length * n_ctx * n_seq))
             for distance in range(1, n_ctx):
                 grad_copy(peer(distance), me).start()
             own_copy.start()
@@ -467,9 +469,8 @@
     for distance in range(1, n_groups):
         target = group_peer(distance)
         hop_copy(hop_up, target, my_group).wait_send()
-        cross_copy(target, my_group).wait_send()
-    for distance in range(1, n_seq):
-        part_copy(seq_peer(distance), my_seq).wait_send()
+    for group, seq in counterparts:
+        cross_copy(group_peer(group), seq_peer(seq), my_slot).wait_send()
 
 
 def writer(
@@ -536,13 +537,12 @@
         + [
             tiles(n_tiles, 2), tiles(LOCAL, per_owner, 2), tiles(LOCAL, per_owner, 2), tiles(n_tiles, 2),
             tiles(per_owner), tiles(per_owner), tiles(n_groups, per_owner),
-            tiles(per_owner), tiles(n_groups, per_sum), tiles(n_tiles), tiles(n_ctx, per_sum),
-            tiles(n_seq, per_sum), tiles(per_sum),
+            tiles(per_owner), tiles(n_groups * n_seq, per_sum), tiles(n_tiles), tiles(n_ctx, per_sum), tiles(per_sum),
         ]
         + [pltpu.SemaphoreType.DMA((LOCAL, owner_pieces)) for _ in range(4)]
-        + [pltpu.SemaphoreType.DMA((n_groups,)) for _ in range(4)]
+        + [pltpu.SemaphoreType.DMA((n_groups,)) for _ in range(2)]
+        + [pltpu.SemaphoreType.DMA((n_groups * n_seq,)) for _ in range(2)]
         + [pltpu.SemaphoreType.DMA((n_ctx,)) for _ in range(4)]
-        + [pltpu.SemaphoreType.DMA((n_seq,)) for _ in range(2)]
         + [pltpu.SemaphoreType.DMA((4, n_parts)), pltpu.SemaphoreType.DMA],
         compiler_params=pltpu.CompilerParams(
             collective_id=0, has_side_effects=True, vmem_limit_bytes=820 * 64 * 1024

time: 32.5 us -> 30.7 us (0.945)
  Pallas kernels: 30.7 us -> 28.9 us
    pallas_call x1, Pallas kernels: 29 us -> 27.2 us  [on_device(): pl.pallas_call(functools.partial(kernel, n_ctx, n_seq, n_parts), out_shap...]
where the time goes in v5:
time: 30.7 us; the launch traced here: 30.5 us
  Pallas kernels  28.9 us (94%)
  other arithmetic  0.99 us (3%)
  between operations  0.64 us (2%)
    pallas_call x1, Pallas kernels, on_device(): pl.pallas_call(functools.partial(kernel, n_ctx, n_seq, n_parts), out_shap...  27.2 us
    pallas_call x1, Pallas kernels, on_device(): pl.pallas_call(writer, out_shape=[signal] * 4 + [jax.ShapeDtypeStruct((mo...  1.68 us
    concatenate x1, other arithmetic, on_device(): jnp.concatenate([decay_rates.T, residues.T], axis=0)  0.99 us

profile of v5, /device:TPU:0, one launch (start us, length us, event | category | flops | bytes accessed | tf_op | source)
XLA Modules:
  0.0 30.5 jit_solution(5843597548432075784)
XLA Ops:
  0.6 1.0 %pad_maximum_fusion.param_ref = f32[32,2048]{1,0:T(8,128)S(1)} fusion(f32[16,2048]{1,0:T(8,128)} %bitcast.15, f32[16,2048]{1,0:T(8,128)} %bitcast.16), kind=kLoop, calls=%fused_computation | loop fusion | flops 65536 | bytes 524288 | tf_op jit(solution)/shard_map/concatenate | solution.py:552
  1.6 27.2 %modal_states.1 = (bf16[128,2048]{1,0:T(8,128)(2,1)S(1)}, bf16[128,2048]{1,0:T(8,128)(2,1)S(1)}, bf16[128,2048]{1,0:T(8,128)(2,1)S(1)}, bf16[128,2048]{1,0:T(8,128)(2,1)S(1)}, f32[32,8,128]{2,1,0:T(8,128)S(1)}) custom-call(bf16[128,2048]{1,0:T(8,128)(2,1)} %bitcast.11, bf16[128,2048]{1,0:T(8,128)(2,1)} %bitcast.12, bf16[128,2048]{1,0:T(8,128)(2,1)} %bitcast.13, ...), custom_call_target="tpu_custom_call" | custom-call | flops 100000000 | bytes 4500000 | tf_op jit(solution)/shard_map/modal_states/pallas_call | solution.py:526
  28.8 1.7 %token_order.1 = (bf16[128,2048]{1,0:T(8,128)(2,1)}, bf16[128,2048]{1,0:T(8,128)(2,1)}, bf16[128,2048]{1,0:T(8,128)(2,1)}, bf16[128,2048]{1,0:T(8,128)(2,1)}, f32[16,2048]{1,0:T(8,128)}) custom-call(bf16[128,2048]{1,0:T(8,128)(2,1)S(1)} %get-tuple-element.15.out_p, bf16[128,2048]{1,0:T(8,128)(2,1)S(1)} %get-tuple-element.16.grad_query_p, ...), custom_call_target="tpu_custom_call" | custom-call | flops 300000000 | bytes 4500000 | tf_op jit(solution)/shard_map/token_order/pallas_call | solution.py:553

commit v6 on v5

--- a/solution.py
+++ b/solution.py
@@ -37,7 +37,7 @@
     n_ctx, n_seq, n_parts, query_hbm, key_hbm, value_hbm, cot_hbm, param_ref,
     out, grad_query, grad_key, grad_value, grad_all,
     query, key, value, cot,
-    query_p, key_p, value_p, cot_p, mix_p, adj_p, conv_p, back_p, before, after, up_turn, down_turn,
+    query_p, key_p, value_p, cot_p, mix_p, adj_p, conv_p, back_p, before, after, up_turn, down_turn, mix_even, adj_even, mix_odd, adj_odd,
     lam_row, lam16_row, weight_row, rate_tile, scale_tile,
     state_out, state_in, carry_out, carry_in, hop_up, hop_down, hop_in,
     cross_out, cross_in, lag_out, lag_in, grad_own,
@@ -69,9 +69,12 @@
         target = (key, value, query, cot)[index]
         return pltpu.make_async_copy(source.at[:, cols], target.at[:, cols], load_sem.at[index, place])
 
-    for place in range(n_parts):
+    def piece_at(index):
+        return lax.rem(owner_pieces * (my_local + 1) + index, n_pieces)
+
+    for order in range(n_pieces):
         for index in range(4):
-            load(index, place).start()
+            load(index, piece_at(order)).start()
 
     def peer(distance):
         return lax.rem(me + distance, n_ctx)
@@ -144,10 +147,12 @@
 
     to_steps = step_order(length, steps, False)
 
-    def turn(place, _):
-        cols = pl.ds(pl.multiple_of(place * part, LANES), part)
+    def take(place):
         for index in range(4):
             load(index, place).wait()
+
+    def turn(place, mix_now, adj_now):
+        cols = pl.ds(pl.multiple_of(place * part, LANES), part)
         key_here, value_here, query_here, cot_here = [
             jnp.dot(to_steps, ref[:, cols], preferred_element_type=F32) for ref in (key, value, query, cot)
         ]
@@ -162,9 +167,8 @@
             cot_p[block] = cot_here[:, lanes]
             mix_p[block] = mixed[:, lanes]
             adj_p[block] = adjoint[:, lanes]
-        return 0
-
-    lax.fori_loop(0, n_parts, turn, 0)
+            mix_now[inner] = mixed[:, lanes]
+            adj_now[inner] = adjoint[:, lanes]
 
     def wide(ref, block, mode):
         return jnp.broadcast_to(ref[block, pl.ds(mode, 1), :], (SUB, LANES))
@@ -183,13 +187,13 @@
     def cut(array):
         return [array[step * SUB:(step + 1) * SUB] for step in range(steps)]
 
-    def states_of(block, inner):
+    def states_of(block, inner, mix_now, adj_now):
         for half in range(halves):
             lams = [wide(lam_row, block, half * SUB + mode) for mode in range(SUB)]
-            lasts = [rows_at(mix_p, block, 0)] * SUB
-            firsts = [rows_at(adj_p, block, steps - 1)] * SUB
+            lasts = [rows_at(mix_now, inner, 0)] * SUB
+            firsts = [rows_at(adj_now, inner, steps - 1)] * SUB
             for step in range(1, steps):
-                mix, adj = rows_at(mix_p, block, step), rows_at(adj_p, block, steps - 1 - step)
+                mix, adj = rows_at(mix_now, inner, step), rows_at(adj_now, inner, steps - 1 - step)
                 lasts = [have * lam + mix for have, lam in zip(lasts, lams)]
                 firsts = [have * lam + adj for have, lam in zip(firsts, lams)]
             for mode in range(SUB):
@@ -214,28 +218,44 @@
                 state = state * lam16 + firsts[chunk]
             state_out[tile, 1] = state
 
+    def send_state(piece):
+        owner, place = piece // owner_pieces, lax.rem(piece, owner_pieces)
+
+        @pl.when(owner != my_local)
+        def _():
+            state_copy(owner, place, my_local).start()
+
+        @pl.when(owner == my_local)
+        def _():
+            state_in[my_local, pl.ds(place * piece_tiles, piece_tiles)] = state_out[pl.ds(piece * piece_tiles, piece_tiles)]
+
+    even, odd = (mix_even, adj_even), (mix_odd, adj_odd)
+
+    def first_piece(order, now, later, last=False):
+        piece = piece_at(order)
+        if not last:
+            following = piece_at(order + 1)
+            take(following)
+            turn(following, *later)
+        for inner in range(piece_blocks):
+            states_of(piece * piece_blocks + inner, inner, *now)
+
+        @pl.when(order == 0)
+        def _():
+            pl.semaphore_wait(barrier, n_ctx - 1 + (n_seq - 1) * n_groups)
+
+        send_state(piece)
+
     def first_pass(index, _):
-        piece = lax.rem(owner_pieces * (my_local + 1) + index, n_pieces)
-        for inner in range(piece_blocks):
-            states_of(piece * piece_blocks + inner, inner)
-
-        @pl.when(index == 0)
-        def _():
-            pl.semaphore_wait(barrier, n_ctx - 1 + (n_seq - 1) * n_groups)
-
-        owner, place = piece // owner_pieces, lax.rem(piece, owner_pieces)
-
-        @pl.when(owner != my_local)
-        def _():
-            state_copy(owner, place, my_local).start()
-
-        @pl.when(owner == my_local)
-        def _():
-            state_in[my_local, pl.ds(place * piece_tiles, piece_tiles)] = state_out[pl.ds(piece * piece_tiles, piece_tiles)]
-
+        first_piece(2 * index, even, odd)
+        first_piece(2 * index + 1, odd, even)
         return 0
 
-    lax.fori_loop(0, n_pieces, first_pass, 0)
+    take(piece_at(0))
+    turn(piece_at(0), *even)
+    lax.fori_loop(0, n_pieces // 2 - 1, first_pass, 0)
+    first_piece(n_pieces - 2, even, odd)
+    first_piece(n_pieces - 1, odd, even, last=True)
 
     def lag_terms(block):
         mix = cut(mix_p[block])
@@ -275,7 +295,7 @@
         for step in range(steps):
             back_p[block, step * SUB:(step + 1) * SUB, :] = totals[step]
     def lag_pass(index, _):
-        piece = lax.rem(owner_pieces * (my_local + 1) + index, n_pieces)
+        piece = piece_at(index)
         for inner in range(piece_blocks):
             lag_terms(piece * piece_blocks + inner)
         for inner in range(piece_tiles // per_sum):
@@ -435,7 +455,7 @@
         for inner in range(piece_blocks):
             finish((owner * owner_pieces + place) * piece_blocks + inner, inner)
 
-        @pl.when(index == n_pieces // 2)
+        @pl.when(index == n_pieces // 4)
         def _():
             for group, seq in counterparts:
                 source, source_seq = group_peer(n_groups - group), seq_peer(n_seq - seq)
@@ -521,7 +541,7 @@
     signal = jax.ShapeDtypeStruct((length, channels), jnp.bfloat16)
     hbm = pl.BlockSpec(memory_space=pltpu.HBM)
     vmem = pl.BlockSpec(memory_space=pltpu.VMEM)
-    n_parts = 4
+    n_parts = n_blocks // piece_blocks
     wide_rows = [pltpu.VMEM((length, channels), jnp.bfloat16) for _ in range(4)]
     results = pl.pallas_call(
         functools.partial(kernel, n_ctx, n_seq, n_parts),
@@ -532,6 +552,7 @@
         + [rows() for _ in range(8)]
         + [tiles(n_tiles, SUB), tiles(n_tiles, SUB)]
         + [tiles(piece_blocks, halves, SUB) for _ in range(2)]
+        + [pltpu.VMEM((piece_blocks, length, LANES), F32) for _ in range(4)]
         + [pltpu.VMEM((n_blocks, modes, LANES), F32) for _ in range(3)]
         + [tiles(n_tiles), tiles(n_tiles)]
         + [
@@ -557,7 +578,7 @@
         out_specs=[hbm] * 5,
         scratch_shapes=[
             pltpu.VMEM((4 * length, channels), jnp.bfloat16), pltpu.VMEM((modes, channels), F32),
-            pltpu.SemaphoreType.DMA((4, n_parts)), pltpu.SemaphoreType.DMA,
+            pltpu.SemaphoreType.DMA((4, 4)), pltpu.SemaphoreType.DMA,
         ],
         compiler_params=pltpu.CompilerParams(vmem_limit_bytes=16 * 1024 * 1024),
         cost_estimate=pl.CostEstimate(flops=300_000_000, bytes_accessed=4_500_000, transcendentals=0),

time: 30.7 us -> 32.1 us (1.046)
  Pallas kernels: 28.9 us -> 30.3 us
    pallas_call x1, Pallas kernels: 27.2 us -> 28.6 us  [on_device(): pl.pallas_call(functools.partial(kernel, n_ctx, n_seq, n_parts), out_shap...]
where the time goes in v6:
time: 32.1 us; the launch traced here: 31.9 us
  Pallas kernels  30.3 us (94%)
  other arithmetic  0.99 us (3%)
  between operations  0.64 us (2%)
    pallas_call x1, Pallas kernels, on_device(): pl.pallas_call(functools.partial(kernel, n_ctx, n_seq, n_parts), out_shap...  28.6 us
    pallas_call x1, Pallas kernels, on_device(): pl.pallas_call(writer, out_shape=[signal] * 4 + [jax.ShapeDtypeStruct((mo...  1.68 us
    concatenate x1, other arithmetic, on_device(): jnp.concatenate([decay_rates.T, residues.T], axis=0)  0.99 us

profile of v6, /device:TPU:0, one launch (start us, length us, event | category | flops | bytes accessed | tf_op | source)
XLA Modules:
  0.0 31.9 jit_solution(4477334237507087054)
XLA Ops:
  0.6 1.0 %pad_maximum_fusion.param_ref = f32[32,2048]{1,0:T(8,128)S(1)} fusion(f32[16,2048]{1,0:T(8,128)} %bitcast.15, f32[16,2048]{1,0:T(8,128)} %bitcast.16), kind=kLoop, calls=%fused_computation | loop fusion | flops 65536 | bytes 524288 | tf_op jit(solution)/shard_map/concatenate | solution.py:573
  1.6 28.6 %modal_states.1 = (bf16[128,2048]{1,0:T(8,128)(2,1)S(1)}, bf16[128,2048]{1,0:T(8,128)(2,1)S(1)}, bf16[128,2048]{1,0:T(8,128)(2,1)S(1)}, bf16[128,2048]{1,0:T(8,128)(2,1)S(1)}, f32[32,8,128]{2,1,0:T(8,128)S(1)}) custom-call(bf16[128,2048]{1,0:T(8,128)(2,1)} %bitcast.11, bf16[128,2048]{1,0:T(8,128)(2,1)} %bitcast.12, bf16[128,2048]{1,0:T(8,128)(2,1)} %bitcast.13, ...), custom_call_target="tpu_custom_call" | custom-call | flops 100000000 | bytes 4500000 | tf_op jit(solution)/shard_map/modal_states/pallas_call | solution.py:546
  30.2 1.7 %token_order.1 = (bf16[128,2048]{1,0:T(8,128)(2,1)}, bf16[128,2048]{1,0:T(8,128)(2,1)}, bf16[128,2048]{1,0:T(8,128)(2,1)}, bf16[128,2048]{1,0:T(8,128)(2,1)}, f32[16,2048]{1,0:T(8,128)}) custom-call(bf16[128,2048]{1,0:T(8,128)(2,1)S(1)} %get-tuple-element.15.out_p, bf16[128,2048]{1,0:T(8,128)(2,1)S(1)} %get-tuple-element.16.grad_query_p, ...), custom_call_target="tpu_custom_call" | custom-call | flops 300000000 | bytes 4500000 | tf_op jit(solution)/shard_map/token_order/pallas_call | solution.py:574

commit v7 on v5

--- a/solution.py
+++ b/solution.py
@@ -435,7 +435,7 @@
         for inner in range(piece_blocks):
             finish((owner * owner_pieces + place) * piece_blocks + inner, inner)
 
-        @pl.when(index == n_pieces // 2)
+        @pl.when(index == n_pieces // 8)
         def _():
             for group, seq in counterparts:
                 source, source_seq = group_peer(n_groups - group), seq_peer(n_seq - seq)

time: 30.7 us -> 30.4 us (level)
  no operation moved by 1% of the time
where the time goes in v7:
time: 30.4 us; the launch traced here: 30.3 us
  Pallas kernels  28.6 us (94%)
  other arithmetic  0.99 us (3%)
  between operations  0.64 us (2%)
    pallas_call x1, Pallas kernels, on_device(): pl.pallas_call(functools.partial(kernel, n_ctx, n_seq, n_parts), out_shap...  27 us
    pallas_call x1, Pallas kernels, on_device(): pl.pallas_call(writer, out_shape=[signal] * 4 + [jax.ShapeDtypeStruct((mo...  1.67 us
    concatenate x1, other arithmetic, on_device(): jnp.concatenate([decay_rates.T, residues.T], axis=0)  0.99 us

profile of v7, /device:TPU:0, one launch (start us, length us, event | category | flops | bytes accessed | tf_op | source)
XLA Modules:
  0.0 30.3 jit_solution(17152879380398596085)
XLA Ops:
  0.6 1.0 %pad_maximum_fusion.param_ref = f32[32,2048]{1,0:T(8,128)S(1)} fusion(f32[16,2048]{1,0:T(8,128)} %bitcast.15, f32[16,2048]{1,0:T(8,128)} %bitcast.16), kind=kLoop, calls=%fused_computation | loop fusion | flops 65536 | bytes 524288 | tf_op jit(solution)/shard_map/concatenate | solution.py:552
  1.6 27.0 %modal_states.1 = (bf16[128,2048]{1,0:T(8,128)(2,1)S(1)}, bf16[128,2048]{1,0:T(8,128)(2,1)S(1)}, bf16[128,2048]{1,0:T(8,128)(2,1)S(1)}, bf16[128,2048]{1,0:T(8,128)(2,1)S(1)}, f32[32,8,128]{2,1,0:T(8,128)S(1)}) custom-call(bf16[128,2048]{1,0:T(8,128)(2,1)} %bitcast.11, bf16[128,2048]{1,0:T(8,128)(2,1)} %bitcast.12, bf16[128,2048]{1,0:T(8,128)(2,1)} %bitcast.13, ...), custom_call_target="tpu_custom_call" | custom-call | flops 100000000 | bytes 4500000 | tf_op jit(solution)/shard_map/modal_states/pallas_call | solution.py:526
  28.6 1.7 %token_order.1 = (bf16[128,2048]{1,0:T(8,128)(2,1)}, bf16[128,2048]{1,0:T(8,128)(2,1)}, bf16[128,2048]{1,0:T(8,128)(2,1)}, bf16[128,2048]{1,0:T(8,128)(2,1)}, f32[16,2048]{1,0:T(8,128)}) custom-call(bf16[128,2048]{1,0:T(8,128)(2,1)S(1)} %get-tuple-element.15.out_p, bf16[128,2048]{1,0:T(8,128)(2,1)S(1)} %get-tuple-element.16.grad_query_p, ...), custom_call_target="tpu_custom_call" | custom-call | flops 300000000 | bytes 4500000 | tf_op jit(solution)/shard_map/token_order/pallas_call | solution.py:553
